TPU v7x, 32 devices: a whole 2x2x4 slice. The times are simulated.
32 devices in a mesh: seq: 8 (over y, x, core), head: 4 (over z).
Axes of the slice: x: 2, y: 2, z: 4, core: 2. Of those that a mesh axis runs over, the one named last changes fastest.
Arguments:
- queries: bfloat16 [4096, 3072], P(('seq', 'head')), may hold values from -8 to 8
- key_vectors: bfloat16 [4096, 3072], P(('seq', 'head')), may hold values from -8 to 8
- value_vectors: bfloat16 [4096, 3072], P(('seq', 'head')), may hold values from -6 to 6
- block_mask: int32 [24, 32, 32], P('head'), may hold values from 0 to 1, as said below
- layout: int32 [32], replicated, may hold values from 0 to 31, as said below
Outputs:
- attended: bfloat16 [4096, 3072], P(('seq', 'head'))
Inputs may be any that keep to these rules, and one draw needn't show every extreme that they name: block_mask[h, c, c] = 1 for every head h and block c. `layout`: a permutation of the block numbers.
All inputs are finite; a program needn't handle non-finite values.
Results may differ from a plain program's by a relative error of at most 0.0035.
Values may be sent and summed in bfloat16 or wider, within the bound.
No kernel may reach another device: no remote copies, remote signals or barrier semaphores. Data moves between devices by JAX's collectives and lax.ppermute only.
A program may use at most 128 MiB of HBM per device.

v0:
```python
import math

import jax
import jax.numpy as jnp
from jax import lax
from jax.experimental import pallas as pl
from jax.experimental.pallas import tpu as pltpu
from jax.sharding import PartitionSpec as P

HEAD_DIM = 128
BLOCK = 128
EXP2_SCALE = math.log2(math.e) / math.sqrt(HEAD_DIM)
KERNEL_VMEM = 32 * 2**20
SCORE_BYTES = 8 * 2**20


def head_lane(place_ref, way, other, turn, shape):
    cores, turns = shape
    core = place_ref[0] ^ other if cores > 1 else 0
    head = ((place_ref[1] ^ way) * cores + core) * turns + turn
    return pl.ds(pl.multiple_of(head * HEAD_DIM, HEAD_DIM), HEAD_DIM)


def in_vmem(body, out_shape, name, place, *operands):
    return pl.pallas_call(
        body,
        in_specs=[pl.BlockSpec(memory_space=pltpu.SMEM)]
        + [pl.BlockSpec(memory_space=pltpu.VMEM)] * len(operands),
        out_specs=jax.tree.map(lambda _: pl.BlockSpec(memory_space=pltpu.VMEM), out_shape),
        out_shape=out_shape,
        name=name,
    )(place, *operands)


def pack_twin(place, sources, parts, ways, shape):
    rows = sources[0].shape[0]

    def body(place_ref, *refs):
        for way in range(ways):
            for part, (source, turn) in enumerate(parts):
                lanes = head_lane(place_ref, way, 1, turn, shape)
                refs[-1][way, part] = refs[source][:, lanes]

    out = jax.ShapeDtypeStruct((ways, len(parts), rows, HEAD_DIM), sources[0].dtype)
    return in_vmem(body, out, "pack_twin", place, *sources)


def pack(place, sources, twin, messages, ways, shape):
    cores, _ = shape
    rows = sources[0].shape[0]
    operands = [*sources] + ([twin] if cores > 1 else [])

    def body(place_ref, *refs):
        ins, outs = refs[: len(operands)], refs[len(operands) :]
        offset = 0
        for at, parts in enumerate(messages):
            for way in range(ways):
                for part, (source, turn) in enumerate(parts):
                    lanes = head_lane(place_ref, way, 0, turn, shape)
                    outs[at * ways + way][0, part] = ins[source][:, lanes]
                    if cores > 1:
                        outs[at * ways + way][1, part] = ins[-1][way, offset + part]
            offset += len(parts)

    out = [
        jax.ShapeDtypeStruct((cores, len(parts), rows, HEAD_DIM), sources[0].dtype)
        for parts in messages
        for _ in range(ways)
    ]
    packed = in_vmem(body, out, "pack", place, *operands)
    return [packed[at * ways : (at + 1) * ways] for at in range(len(messages))]


def unpack(place, pieces, twins, shape):
    cores, turns = shape
    ways, rows = len(pieces[0]), pieces[0][0].shape[2]
    flat = [piece for group in pieces for piece in group]
    operands = flat + (twins if cores > 1 else [])

    def body(place_ref, *refs):
        for turn in range(turns):
            for way in range(ways):
                lanes = head_lane(place_ref, way, 0, turn, shape)
                refs[-1][:, lanes] = refs[turn * ways + way][0, 0]
                if cores > 1:
                    lanes = head_lane(place_ref, way, 1, turn, shape)
                    refs[-1][:, lanes] = refs[len(flat) + turn][way]

    out = jax.ShapeDtypeStruct((rows, ways * cores * turns * HEAD_DIM), flat[0].dtype)
    return in_vmem(body, out, "unpack", place, *operands)


def attend(place, layout, query_ids, key_ids, block_mask, turn, queries, parts, extra, shape):
    cores, turns = shape
    ways, rows = len(queries), queries[0].shape[2]
    query_part = queries[0].shape[1] - 1
    units = ways * cores * rows // BLOCK
    blocks = sum(part.shape[0] * part.shape[1] for part in parts) * cores * rows // BLOCK
    width = blocks * BLOCK
    group = max(1, min(units, SCORE_BYTES // (4 * BLOCK * width)))
    while units % group:
        group -= 1
    lots = []
    for which, part in enumerate(parts):
        held = part.shape[1] * cores * rows // BLOCK
        for member in range(part.shape[0]):
            lots += [
                (which, member, first, min(4, held - first)) for first in range(0, held, 4)
            ]

    def body(place_ref, layout_ref, query_ids_ref, key_ids_ref, mask_ref, *refs):
        query_refs, part_refs = refs[:ways], refs[ways : ways + len(parts)]
        extra_refs, out_refs = refs[ways + len(parts) : -3 - ways], refs[-3 - ways : -3]
        scores, asked, answered = refs[-3:]
        for way in range(ways):
            for other in range(cores):
                at = (way * cores + other) * rows
                asked[at : at + rows] = query_refs[way][other, query_part]

        def some(which, part, member, first, count):
            whole = part_refs[part][member, :, :, which].reshape(-1, HEAD_DIM)
            return whole[first * BLOCK : (first + count) * BLOCK]

        def step(lot, carry):
            tile = asked[pl.ds(pl.multiple_of(lot * group * BLOCK, BLOCK), group * BLOCK)]
            mask_rows = [layout_ref[query_ids_ref[lot * group + at]] for at in range(group)]
            maxima = [None] * group
            block = 0
            for lot_at in lots:
                found = lax.dot_general(
                    tile,
                    some(0, *lot_at),
                    (((1,), (1,)), ((), ())),
                    preferred_element_type=jnp.float32,
                )
                for unit in range(lot_at[-1]):
                    column = layout_ref[key_ids_ref[block]]
                    for at in range(group):
                        allowed = mask_ref[0, mask_rows[at], column] > 0
                        bias = jnp.where(allowed, jnp.float32(0), jnp.float32(-jnp.inf))
                        piece = (
                            found[
                                at * BLOCK : (at + 1) * BLOCK, unit * BLOCK : (unit + 1) * BLOCK
                            ]
                            + bias
                        )
                        scores[
                            at * BLOCK : (at + 1) * BLOCK, block * BLOCK : (block + 1) * BLOCK
                        ] = piece
                        maxima[at] = piece if maxima[at] is None else jnp.maximum(maxima[at], piece)
                    block += 1
            for at in range(group):
                shift = jnp.max(maxima[at], axis=1, keepdims=True) * EXP2_SCALE
                total = accum = None
                block = 0
                for lot_at in lots:
                    count = lot_at[-1]
                    wide = scores[
                        at * BLOCK : (at + 1) * BLOCK, block * BLOCK : (block + count) * BLOCK
                    ]
                    probs = jnp.exp2(wide * EXP2_SCALE - shift)
                    for unit in range(count):
                        piece = probs[:, unit * BLOCK : (unit + 1) * BLOCK]
                        total = piece if total is None else total + piece
                    product = jnp.dot(
                        probs.astype(jnp.bfloat16),
                        some(1, *lot_at),
                        preferred_element_type=jnp.float32,
                    )
                    accum = product if accum is None else accum + product
                    block += count
                total = jnp.sum(total, axis=1, keepdims=True)
                spot = pl.multiple_of((lot * group + at) * BLOCK, BLOCK)
                answered[pl.ds(spot, BLOCK)] = (accum / total).astype(jnp.bfloat16)
            return carry

        lax.fori_loop(0, units // group, step, 0)
        for way in range(ways):
            for other in range(cores):
                at = (way * cores + other) * rows
                out_refs[way][other, 0] = answered[at : at + rows]
                if extra:
                    out_refs[way][other, 1] = extra_refs[way][other, 0]

    whole = pl.BlockSpec(memory_space=pltpu.VMEM)
    return pl.pallas_call(
        body,
        grid_spec=pltpu.PrefetchScalarGridSpec(
            num_scalar_prefetch=4,
            grid=(1,),
            in_specs=[
                pl.BlockSpec(
                    (1, blocks, blocks),
                    lambda step, place, *_: (place[0] * turns + turn, 0, 0),
                    memory_space=pltpu.SMEM,
                )
            ]
            + [whole] * (ways + len(parts) + len(extra)),
            out_specs=[whole] * ways,
            scratch_shapes=[
                pltpu.VMEM((group * BLOCK, width), jnp.float32),
                pltpu.VMEM((units * BLOCK, HEAD_DIM), jnp.bfloat16),
                pltpu.VMEM((units * BLOCK, HEAD_DIM), jnp.bfloat16),
            ],
        ),
        out_shape=[
            jax.ShapeDtypeStruct((cores, 2 if extra else 1, rows, HEAD_DIM), jnp.bfloat16)
        ]
        * ways,
        compiler_params=pltpu.CompilerParams(vmem_limit_bytes=KERNEL_VMEM),
        cost_estimate=pl.CostEstimate(
            flops=40 * units * BLOCK * width * HEAD_DIM,
            bytes_accessed=4 * width * HEAD_DIM,
            transcendentals=units * BLOCK * width,
        ),
        name="attend",
    )(place, layout, query_ids, key_ids, block_mask, *queries, *parts, *extra)


def after(array, *others):
    return lax.optimization_barrier((array, *others))[0]


def per_device(queries, key_vectors, value_vectors, block_mask, layout):
    ways, seq_count = lax.axis_size("head"), lax.axis_size("seq")
    seq, way_here = lax.axis_index("seq"), lax.axis_index("head")
    rows, width = queries.shape
    heads_here = width // HEAD_DIM // ways
    relay = seq_count == 8 and heads_here % 2 == 0
    cores = 2 if relay else 1
    turns = heads_here // cores
    shape = (cores, turns)
    assert BLOCK % rows == 0 and ways & (ways - 1) == 0 and ways * rows % BLOCK == 0
    fold = BLOCK // rows
    assert fold == 1 or cores == 1
    chip, core = seq // cores, seq % cores
    place = jnp.stack([core, way_here]).astype(jnp.int32)
    near = [(s, s ^ (4 if s & 1 else 2)) for s in range(8)]
    far = [(s, s ^ (2 if s & 1 else 4)) for s in range(8)]
    twins = [(s, s ^ 1) for s in range(8)]
    if relay:
        flip = 1 + core
        chips = jnp.stack([chip, chip ^ flip, chip ^ 3 ^ flip, chip ^ 3])
    else:
        chips = jnp.arange(seq_count)

    def block_ids(of_chips):
        of_core = of_chips[:, None, None] * cores + (core ^ jnp.arange(cores))[None, None, :]
        of_way = (way_here ^ jnp.arange(0, ways, fold))[None, :, None]
        return ((of_core * ways + of_way) // fold).reshape(-1).astype(jnp.int32)

    query_ids, key_ids = block_ids(chip[None]), block_ids(chips)

    def swap(array, way):
        return lax.ppermute(array, "head", [(z, z ^ way) for z in range(ways)])

    def send(array, pairs):
        return lax.ppermute(array, "seq", pairs)

    sources = (key_vectors, value_vectors, queries)
    messages = [
        [(0, turn), (1, turn)] + ([(2, turn - 1)] if turn else []) for turn in range(turns)
    ]
    messages.append([(2, turns - 1)])
    rest = [part for parts in messages[1:] for part in parts]
    if relay:
        first_twin = send(pack_twin(place, sources[:2], messages[0], ways, shape), twins)
        sent = pack(place, sources[:2], first_twin, messages[:1], ways, shape)
        rest_twin = pack_twin(place, sources, rest, ways, shape)
        rest_twin = send(after(rest_twin, sent[0][0]), twins)
    else:
        sent, rest_twin = pack(place, sources[:2], None, messages[:1], ways, shape), None
    sent += pack(place, sources, rest_twin, messages[1:], ways, shape)

    held, shared, pieces, outs, returned, back = [], [], [], [], [], []

    def exchange(turn):
        got = [sent[turn][0]]
        for way in range(1, ways):
            message = sent[turn][way]
            if turn:
                message = after(message, held[turn - 1][way])
            if turn > 1:
                message = after(message, *pieces[turn - 2][-2:])
            got.append(swap(message, way))
        held.append(got)

    def gather(turn):
        got = list(held[turn])
        earlier = pieces[turn - 1][-2:] if turn else [sent[1][0]]
        got[0] = after(got[0], *earlier)
        joined = jnp.stack([piece[:, :2] for piece in got], axis=0)
        shared.append(joined)
        if not relay:
            return [lax.all_gather(joined, "seq", axis=0)]
        first, second = send(joined, near), send(joined, far)
        half = ways // 2
        parts = [joined, first, second]

        def onward(outs):
            waits = list(outs) + (returned[0] if turn == turns - 1 else [])
            one, two = lax.optimization_barrier((first[:half], second[half:], *waits))[:2]
            if turn == turns - 1:
                sidelong.extend([one, two])
            return [part[None] for part in parts + [send(one, far), send(two, near)]]

        return onward

    def bring_back(turn):
        result = outs[turn]
        if turn + 2 < turns:
            result = lax.optimization_barrier((*result, shared[turn + 2]))[:-1]
        elif turn + 1 < turns:
            result = lax.optimization_barrier((*result, *sidelong))[: len(result)]
        result = [result[0]] + [swap(result[way], way) for way in range(1, ways)]
        returned.append(result)
        if relay:
            back.append(send(jnp.stack([piece[1, 0] for piece in result]), twins))

    sidelong = []
    exchange(0)
    pieces.append(gather(0))
    if relay:
        pieces[0] = pieces[0]([])
    exchange(1)
    for turn in range(turns):
        if turn + 2 < turns:
            exchange(turn + 2)
        parts = list(pieces[turn])
        onward = None
        if turn + 1 < turns:
            onward = gather(turn + 1)
            parts[0] = after(parts[0], shared[turn + 1])
        asked = held[turn + 1] if turn + 1 < turns else returned[0]
        extra = sent[turns] if turn == 0 else []
        outs.append(
            attend(
                place, layout, query_ids, key_ids, block_mask, turn, asked, parts, extra, shape
            )
        )
        if turn and turn + 1 < turns:
            bring_back(turn - 1)
        if turn + 1 < turns:
            pieces.append(onward(outs[turn]) if relay else onward)
    for turn in range(len(returned), turns):
        bring_back(turn)
    return unpack(place, returned, back, shape)


def solution(mesh):
    placed = (
        P(("seq", "head"), None),
        P(("seq", "head"), None),
        P(("seq", "head"), None),
        P("head", None, None),
        P(),
    )
    return jax.shard_map(
        per_device, mesh=mesh, in_specs=placed, out_specs=P(("seq", "head"), None), check_vma=False
    )
```

profile of v0, /device:TPU:0, one launch (start us, length us, event | category | flops | bytes accessed | tf_op | source)
XLA Modules:
  0.0 132.5 jit_solution(11183703418085759507)
XLA Ops:
  0.0 0.6 pad_add_fusion.place_ref
  0.6 2.2 %pack_twin.3 = bf16[4,2,128,128]{3,2,1,0:T(8,128)(2,1)} custom-call(s32[2]{0:T(128)} %pad_add_fusion.place_ref, bf16[128,3072]{1,0:T(8,128)(2,1)} %refs_0_.7, bf16[128,3072]{1,0:T(8,128)(2,1)} %refs_1_.7), custom_call_target="tpu_custom_call" | custom-call | tf_op jit(solution)/shard_map/pack_twin/pallas_call | solution.py:25
  2.7 0.5 collective-permute-start
  3.2 2.8 %pack_twin.2 = bf16[4,7,128,128]{3,2,1,0:T(8,128)(2,1)} custom-call(s32[2]{0:T(128)} %pad_add_fusion.place_ref, bf16[128,3072]{1,0:T(8,128)(2,1)} %refs_0_.7, bf16[128,3072]{1,0:T(8,128)(2,1)} %refs_1_.7, bf16[128,3072]{1,0:T(8,128)(2,1)} %refs_2_.3), custom_call_target="tpu_custom_call" | custom-call | tf_op jit(solution)/shard_map/pack_twin/pallas_call | solution.py:25
  6.0 0.7 copy-done.17
  6.7 2.2 %pack.2 = (bf16[2,2,128,128]{3,2,1,0:T(8,128)(2,1)}, bf16[2,2,128,128]{3,2,1,0:T(8,128)(2,1)}, bf16[2,2,128,128]{3,2,1,0:T(8,128)(2,1)}, bf16[2,2,128,128]{3,2,1,0:T(8,128)(2,1)}) custom-call(s32[2]{0:T(128)} %pad_add_fusion.place_ref, bf16[128,3072]{1,0:T(8,128)(2,1)} %refs_0_.7, bf16[128,3072]{1,0:T(8,128)(2,1)} %refs_1_.7, bf16[4,2,128,128]{3,2,1,0:T(8,128)(2,1)} %copy-done.17), custom_call_target="tpu_custom_call" | custom-call | tf_op jit(solution)/shard_map/pack/pallas_call | solution.py:25
  9.1 0.1 add.86
  9.1 0.1 add_multiply_fusion.1
  9.2 3.0 %collective-permute-start.2 = (bf16[2,2,128,128]{3,2,1,0:T(8,128)(2,1)}, bf16[2,2,128,128]{3,2,1,0:T(8,128)(2,1)S(1)}, u32[]{:S(2)}, u32[]{:S(2)}) collective-permute-start(bf16[2,2,128,128]{3,2,1,0:T(8,128)(2,1)} %get-tuple-element.66), channel_id=1, source_target_pairs={{0,1},{1,0},{2,3},{3,2},{4,5},{5,4},{6,7},{7,6},{8,9},{9,8},{10,11... | collective-permute-start | bytes 393224 | tf_op jit(solution)/shard_map/ppermute | solution.py:255
  12.2 2.6 %collective-permute-start.4 = (bf16[2,2,128,128]{3,2,1,0:T(8,128)(2,1)}, bf16[2,2,128,128]{3,2,1,0:T(8,128)(2,1)S(1)}, u32[]{:S(2)}, u32[]{:S(2)}) collective-permute-start(bf16[2,2,128,128]{3,2,1,0:T(8,128)(2,1)} %get-tuple-element.69), channel_id=1, source_target_pairs={{0,2},{1,3},{2,0},{3,1},{4,6},{5,7},{6,4},{7,5},{8,10},{9,11},{10,... | collective-permute-start | bytes 393224 | tf_op jit(solution)/shard_map/ppermute | solution.py:255
  14.8 0.1 add_multiply_fusion
  14.9 1.0 copy-done.15
  15.9 3.2 %pack.3 = (bf16[2,3,128,128]{3,2,1,0:T(8,128)(2,1)}, bf16[2,3,128,128]{3,2,1,0:T(8,128)(2,1)}, bf16[2,3,128,128]{3,2,1,0:T(8,128)(2,1)}, bf16[2,3,128,128]{3,2,1...) custom-call(s32[2]{0:T(128)} %pad_add_fusion.place_ref, ...), custom_call_target="tpu_custom_call" | custom-call | tf_op jit(solution)/shard_map/pack/pallas_call | solution.py:25
  19.1 6.2 %collective-permute-done.4 = bf16[2,2,128,128]{3,2,1,0:T(8,128)(2,1)S(1)} collective-permute-done((bf16[2,2,128,128]{3,2,1,0:T(8,128)(2,1)}, bf16[2,2,128,128]{3,2,1,0:T(8,128)(2,1)S(1)}, u32[]{:S(2)}, u32[]{:S(2)}) %collective-permute-start.4) | collective-permute-done | bytes 131104 | tf_op jit(solution)/shard_map/ppermute | solution.py:255
  25.4 0.1 pad_maximum_fusion
  25.5 1.6 %collective-permute-start.8 = (bf16[4,2,2,128,128]{4,3,2,1,0:T(8,128)(2,1)S(1)}, bf16[4,2,2,128,128]{4,3,2,1,0:T(8,128)(2,1)S(1)}, u32[]{:S(2)}, u32[]{:S(2)}) collective-permute-start(bf16[4,2,2,128,128]{4,3,2,1,0:T(8,128)(2,1)S(1)} %get-tuple-element.123), channel_id=1, source_target_pairs={{0,8},{4,20},{8,0},{12,28},{16,24},{20,4},{24,16},{28,12},{1,9},{5... | collective-permute-start | bytes 1572872 | tf_op jit(solution)/shard_map/ppermute | solution.py:258
  27.1 1.5 %collective-permute-start.9 = (bf16[4,2,2,128,128]{4,3,2,1,0:T(8,128)(2,1)S(1)}, bf16[4,2,2,128,128]{4,3,2,1,0:T(8,128)(2,1)S(1)}, u32[]{:S(2)}, u32[]{:S(2)}) collective-permute-start(bf16[4,2,2,128,128]{4,3,2,1,0:T(8,128)(2,1)S(1)} %get-tuple-element.123), channel_id=1, source_target_pairs={{0,16},{4,12},{8,24},{12,4},{16,0},{20,28},{24,8},{28,20},{1,17},{... | collective-permute-start | bytes 1572872 | tf_op jit(solution)/shard_map/ppermute | solution.py:258
  28.6 0.1 add.87
  28.6 0.1 add.88
  28.7 2.4 %collective-permute-start.7 = (bf16[2,3,128,128]{3,2,1,0:T(8,128)(2,1)S(1)}, bf16[2,3,128,128]{3,2,1,0:T(8,128)(2,1)S(1)}, u32[]{:S(2)}, u32[]{:S(2)}) collective-permute-start(bf16[2,3,128,128]{3,2,1,0:T(8,128)(2,1)S(1)} %copy-done.33), channel_id=1, source_target_pairs={{0,3},{1,2},{2,1},{3,0},{4,7},{5,6},{6,5},{7,4},{8,11},{9,10},{10,... | collective-permute-start | bytes 589832 | tf_op jit(solution)/shard_map/ppermute | solution.py:255
  31.2 0.1 add.97.key_ids_ref
  31.3 1.4 %collective-permute-start.3 = (bf16[2,3,128,128]{3,2,1,0:T(8,128)(2,1)S(1)}, bf16[2,3,128,128]{3,2,1,0:T(8,128)(2,1)S(1)}, u32[]{:S(2)}, u32[]{:S(2)}) collective-permute-start(bf16[2,3,128,128]{3,2,1,0:T(8,128)(2,1)S(1)} %copy-done.31), channel_id=1, source_target_pairs={{0,1},{1,0},{2,3},{3,2},{4,5},{5,4},{6,7},{7,6},{8,9},{9,8},{10,11... | collective-permute-start | bytes 589832 | tf_op jit(solution)/shard_map/ppermute | solution.py:255
  32.7 0.7 collective-permute-start.5
  33.4 5.1 %collective-permute-done.7.refs_3_ = bf16[2,3,128,128]{3,2,1,0:T(8,128)(2,1)S(1)} collective-permute-done((bf16[2,3,128,128]{3,2,1,0:T(8,128)(2,1)S(1)}, bf16[2,3,128,128]{3,2,1,0:T(8,128)(2,1)S(1)}, u32[]{:S(2)}, u32[]{:S(2)}) %collective-permute-start.7) | collective-permute-done | bytes 196640 | tf_op jit(solution)/shard_map/ppermute | solution.py:255
  38.6 0.6 collective-permute-start.10
  39.2 1.5 %collective-permute-start.11 = (bf16[2,2,2,128,128]{4,3,2,1,0:T(8,128)(2,1)S(1)}, bf16[2,2,2,128,128]{4,3,2,1,0:T(8,128)(2,1)S(1)}, u32[]{:S(2)}, u32[]{:S(2)}) collective-permute-start(bf16[2,2,2,128,128]{4,3,2,1,0:T(8,128)(2,1)S(1)} %slice.105), channel_id=1, source_target_pairs={{0,8},{4,20},{8,0},{12,28},{16,24},{20,4},{24,16},{28,12},{1,9},{5... | collective-permute-start | bytes 786440 | tf_op jit(solution)/shard_map/ppermute | solution.py:258
  40.7 6.5 %collective-permute-done.5.refs_2_ = bf16[2,3,128,128]{3,2,1,0:T(8,128)(2,1)S(1)} collective-permute-done((bf16[2,3,128,128]{3,2,1,0:T(8,128)(2,1)S(1)}, bf16[2,3,128,128]{3,2,1,0:T(8,128)(2,1)S(1)}, u32[]{:S(2)}, u32[]{:S(2)}) %collective-permute-start.5) | collective-permute-done | bytes 196640 | tf_op jit(solution)/shard_map/ppermute | solution.py:255
  47.3 0.9 copy-done.7
  48.3 0.1 fusion.1
  48.4 0.6 collective-permute-start.12
  49.0 0.6 collective-permute-start.13
  49.6 2.5 %collective-permute-start.18 = (bf16[2,3,128,128]{3,2,1,0:T(8,128)(2,1)S(1)}, bf16[2,3,128,128]{3,2,1,0:T(8,128)(2,1)S(1)}, u32[]{:S(2)}, u32[]{:S(2)}) collective-permute-start(bf16[2,3,128,128]{3,2,1,0:T(8,128)(2,1)S(1)} %copy-done.30), channel_id=1, source_target_pairs={{0,3},{1,2},{2,1},{3,0},{4,7},{5,6},{6,5},{7,4},{8,11},{9,10},{10,... | collective-permute-start | bytes 589832 | tf_op jit(solution)/shard_map/ppermute | solution.py:255
  52.0 5.3 %collective-permute-start.17 = (bf16[2,3,128,128]{3,2,1,0:T(8,128)(2,1)S(1)}, bf16[2,3,128,128]{3,2,1,0:T(8,128)(2,1)S(1)}, u32[]{:S(2)}, u32[]{:S(2)}) collective-permute-start(bf16[2,3,128,128]{3,2,1,0:T(8,128)(2,1)S(1)} %copy-done.29), channel_id=1, source_target_pairs={{0,2},{1,3},{2,0},{3,1},{4,6},{5,7},{6,4},{7,5},{8,10},{9,11},{10,... | collective-permute-start | bytes 589832 | tf_op jit(solution)/shard_map/ppermute | solution.py:255
  57.4 0.5 copy-done.8
  58.0 9.3 %attend.3 = (bf16[2,2,128,128]{3,2,1,0:T(8,128)(2,1)S(1)}, bf16[2,2,128,128]{3,2,1,0:T(8,128)(2,1)S(1)}, bf16[2,2,128,128]{3,2,1,0:T(8,128)(2,1)S(1)}, bf16[2,2,128,128]{3,2,1,0:T(8,128)(2,1)S(1)}) custom-call(s32[2]{0:T(128)S(1)} %copy-done.8, s32[32]{0:T(128)S(1)} %copy-done.14, s32[8]{0:T(128)S(1)} %add.89.query_ids_ref, s32[32]{0:T(128)S(1)} %add.97.key_ids_ref, ...), custom_call_target="tpu_custom_call" | custom-call | flops 21474836480 | bytes 2097152 | tf_op jit(solution)/shard_map/attend/pallas_call | solution.py:186
  67.4 0.7 collective-permute-start.14
  68.1 1.5 %collective-permute-start.15 = (bf16[2,2,2,128,128]{4,3,2,1,0:T(8,128)(2,1)S(1)}, bf16[2,2,2,128,128]{4,3,2,1,0:T(8,128)(2,1)S(1)}, u32[]{:S(2)}, u32[]{:S(2)}) collective-permute-start(bf16[2,2,2,128,128]{4,3,2,1,0:T(8,128)(2,1)S(1)} %slice.110), channel_id=1, source_target_pairs={{0,8},{4,20},{8,0},{12,28},{16,24},{20,4},{24,16},{28,12},{1,9},{5... | collective-permute-start | bytes 786440 | tf_op jit(solution)/shard_map/ppermute | solution.py:258
  69.7 6.9 %collective-permute-done.14 = bf16[2,2,2,128,128]{4,3,2,1,0:T(8,128)(2,1)S(1)} collective-permute-done((bf16[2,2,2,128,128]{4,3,2,1,0:T(8,128)(2,1)S(1)}, bf16[2,2,2,128,128]{4,3,2,1,0:T(8,128)(2,1)S(1)}, u32[]{:S(2)}, u32[]{:S(2)}) %collective-permute-start.14) | collective-permute-done | bytes 262176 | tf_op jit(solution)/shard_map/ppermute | solution.py:258
  76.6 0.7 collective-permute-done.15
  77.3 0.1 fusion
  77.4 1.5 %collective-permute-start.22 = (bf16[4,2,2,128,128]{4,3,2,1,0:T(8,128)(2,1)S(1)}, bf16[4,2,2,128,128]{4,3,2,1,0:T(8,128)(2,1)S(1)}, u32[]{:S(2)}, u32[]{:S(2)}) collective-permute-start(bf16[4,2,2,128,128]{4,3,2,1,0:T(8,128)(2,1)S(1)} %get-tuple-element.120), channel_id=1, source_target_pairs={{0,8},{4,20},{8,0},{12,28},{16,24},{20,4},{24,16},{28,12},{1,9},{5... | collective-permute-start | bytes 1572872 | tf_op jit(solution)/shard_map/ppermute | solution.py:258
  79.0 1.5 %collective-permute-start.23 = (bf16[4,2,2,128,128]{4,3,2,1,0:T(8,128)(2,1)S(1)}, bf16[4,2,2,128,128]{4,3,2,1,0:T(8,128)(2,1)S(1)}, u32[]{:S(2)}, u32[]{:S(2)}) collective-permute-start(bf16[4,2,2,128,128]{4,3,2,1,0:T(8,128)(2,1)S(1)} %get-tuple-element.120), channel_id=1, source_target_pairs={{0,16},{4,12},{8,24},{12,4},{16,0},{20,28},{24,8},{28,20},{1,17},{... | collective-permute-start | bytes 1572872 | tf_op jit(solution)/shard_map/ppermute | solution.py:258
  80.4 1.6 %collective-permute-start.19 = (bf16[2,2,128,128]{3,2,1,0:T(8,128)(2,1)S(1)}, bf16[2,2,128,128]{3,2,1,0:T(8,128)(2,1)S(1)}, u32[]{:S(2)}, u32[]{:S(2)}) collective-permute-start(bf16[2,2,128,128]{3,2,1,0:T(8,128)(2,1)S(1)} %get-tuple-element.101), channel_id=1, source_target_pairs={{0,1},{1,0},{2,3},{3,2},{4,5},{5,4},{6,7},{7,6},{8,9},{9,8},{10,11... | collective-permute-start | bytes 393224 | tf_op jit(solution)/shard_map/ppermute | solution.py:255
  82.0 1.2 collective-permute-start.20
  83.2 1.6 %collective-permute-start.21 = (bf16[2,2,128,128]{3,2,1,0:T(8,128)(2,1)S(1)}, bf16[2,2,128,128]{3,2,1,0:T(8,128)(2,1)S(1)}, u32[]{:S(2)}, u32[]{:S(2)}) collective-permute-start(bf16[2,2,128,128]{3,2,1,0:T(8,128)(2,1)S(1)} %get-tuple-element.103), channel_id=1, source_target_pairs={{0,3},{1,2},{2,1},{3,0},{4,7},{5,6},{6,5},{7,4},{8,11},{9,10},{10,... | collective-permute-start | bytes 393224 | tf_op jit(solution)/shard_map/ppermute | solution.py:255
  84.8 9.0 %attend.4 = (bf16[2,1,128,128]{3,2,1,0:T(8,128)(2,1)S(1)}, bf16[2,1,128,128]{3,2,1,0:T(8,128)(2,1)S(1)}, bf16[2,1,128,128]{3,2,1,0:T(8,128)(2,1)S(1)}, bf16[2,1,128,128]{3,2,1,0:T(8,128)(2,1)S(1)}) custom-call(s32[2]{0:T(128)S(1)} %copy-done.8, s32[32]{0:T(128)S(1)} %copy-done.14, s32[8]{0:T(128)S(1)} %add.89.query_ids_ref, s32[32]{0:T(128)S(1)} %add.97.key_ids_ref, ...), custom_call_target="tpu_custom_call" | custom-call | flops 21474836480 | bytes 2097152 | tf_op jit(solution)/shard_map/attend/pallas_call | solution.py:186
  94.1 0.7 collective-permute-start.27
  94.9 0.5 collective-permute-start.28
  95.4 1.1 collective-permute-start.24
  96.5 2.3 %collective-permute-start.26 = (bf16[2,1,128,128]{3,2,1,0:T(8,128)(2,1)S(1)}, bf16[2,1,128,128]{3,2,1,0:T(8,128)(2,1)S(1)}, u32[]{:S(2)}, u32[]{:S(2)}) collective-permute-start(bf16[2,1,128,128]{3,2,1,0:T(8,128)(2,1)S(1)} %get-tuple-element.114), channel_id=1, source_target_pairs={{0,3},{1,2},{2,1},{3,0},{4,7},{5,6},{6,5},{7,4},{8,11},{9,10},{10,... | collective-permute-start | bytes 196616 | tf_op jit(solution)/shard_map/ppermute | solution.py:255
  98.8 3.8 %collective-permute-done.26.refs_7_ = bf16[2,1,128,128]{3,2,1,0:T(8,128)(2,1)S(1)} collective-permute-done((bf16[2,1,128,128]{3,2,1,0:T(8,128)(2,1)S(1)}, bf16[2,1,128,128]{3,2,1,0:T(8,128)(2,1)S(1)}, u32[]{:S(2)}, u32[]{:S(2)}) %collective-permute-start.26) | collective-permute-done | bytes 65568 | tf_op jit(solution)/shard_map/ppermute | solution.py:255
  102.6 0.6 collective-permute-start.25
  103.2 4.6 %collective-permute-done.25.refs_6_ = bf16[2,1,128,128]{3,2,1,0:T(8,128)(2,1)S(1)} collective-permute-done((bf16[2,1,128,128]{3,2,1,0:T(8,128)(2,1)S(1)}, bf16[2,1,128,128]{3,2,1,0:T(8,128)(2,1)S(1)}, u32[]{:S(2)}, u32[]{:S(2)}) %collective-permute-start.25) | collective-permute-done | bytes 65568 | tf_op jit(solution)/shard_map/ppermute | solution.py:255
  107.9 0.6 copy-done.20
  108.5 9.2 %attend.5 = (bf16[2,1,128,128]{3,2,1,0:T(8,128)(2,1)S(1)}, bf16[2,1,128,128]{3,2,1,0:T(8,128)(2,1)S(1)}, bf16[2,1,128,128]{3,2,1,0:T(8,128)(2,1)S(1)}, bf16[2,1,128,128]{3,2,1,0:T(8,128)(2,1)S(1)}) custom-call(s32[2]{0:T(128)S(1)} %copy-done.8, s32[32]{0:T(128)S(1)} %copy-done.14, s32[8]{0:T(128)S(1)} %add.89.query_ids_ref, s32[32]{0:T(128)S(1)} %add.97.key_ids_ref, ...), custom_call_target="tpu_custom_call" | custom-call | flops 21474836480 | bytes 2097152 | tf_op jit(solution)/shard_map/attend/pallas_call | solution.py:186
  117.8 0.1 collective-permute-start.29
  117.8 2.8 %collective-permute-start.30 = (bf16[2,1,128,128]{3,2,1,0:T(8,128)(2,1)S(1)}, bf16[2,1,128,128]{3,2,1,0:T(8,128)(2,1)S(1)}, u32[]{:S(2)}, u32[]{:S(2)}) collective-permute-start(bf16[2,1,128,128]{3,2,1,0:T(8,128)(2,1)S(1)} %get-tuple-element.117), channel_id=1, source_target_pairs={{0,2},{1,3},{2,0},{3,1},{4,6},{5,7},{6,4},{7,5},{8,10},{9,11},{10,... | collective-permute-start | bytes 196616 | tf_op jit(solution)/shard_map/ppermute | solution.py:255
  120.6 1.6 %collective-permute-start.31 = (bf16[2,1,128,128]{3,2,1,0:T(8,128)(2,1)S(1)}, bf16[2,1,128,128]{3,2,1,0:T(8,128)(2,1)S(1)}, u32[]{:S(2)}, u32[]{:S(2)}) collective-permute-start(bf16[2,1,128,128]{3,2,1,0:T(8,128)(2,1)S(1)} %get-tuple-element.118), channel_id=1, source_target_pairs={{0,3},{1,2},{2,1},{3,0},{4,7},{5,6},{6,5},{7,4},{8,11},{9,10},{10,... | collective-permute-start | bytes 196616 | tf_op jit(solution)/shard_map/ppermute | solution.py:255
  122.2 4.5 %collective-permute-done.31.refs_11_ = bf16[2,1,128,128]{3,2,1,0:T(8,128)(2,1)S(1)} collective-permute-done((bf16[2,1,128,128]{3,2,1,0:T(8,128)(2,1)S(1)}, bf16[2,1,128,128]{3,2,1,0:T(8,128)(2,1)S(1)}, u32[]{:S(2)}, u32[]{:S(2)}) %collective-permute-start.31) | collective-permute-done | bytes 65568 | tf_op jit(solution)/shard_map/ppermute | solution.py:255
  126.8 0.6 copy-done.23
  127.4 0.6 copy-done.21
  128.0 1.3 collective-permute-done.34.refs_14_
  129.3 0.7 copy-done.27
  130.0 2.5 %unpack.1 = bf16[128,3072]{1,0:T(8,128)(2,1)} custom-call(s32[2]{0:T(128)} %pad_add_fusion.place_ref, bf16[2,2,128,128]{3,2,1,0:T(8,128)(2,1)} %copy-done, bf16[2,2,128,128]{3,2,1,0:T(8,128)(2,1)} %copy-done.1, bf16[2,2,128,128]{3,2,1,0:T(8,128)(2,1)} %copy-done.2, bf16[2,2,128,128]{3,2,1,0:T(8,128)(2,1)} %copy-done.3, bf16[2,1,128,128]{3,2,1,0:T(8,128)(2,1)} %copy-done.4, ...), custom_call_target="tpu_custom_call" | custom-call | tf_op jit(solution)/shard_map/unpack/pallas_call | solution.py:25
  (126 shorter events, 0.8 us)
Async XLA Ops:
  2.7 3.3 %collective-permute-start = (bf16[4,2,128,128]{3,2,1,0:T(8,128)(2,1)}, bf16[4,2,128,128]{3,2,1,0:T(8,128)(2,1)S(1)}, u32[]{:S(2)}, u32[]{:S(2)}) collective-permute-start(bf16[4,2,128,128]{3,2,1,0:T(8,128)(2,1)} %pack_twin.3), channel_id=1, source_target_pairs={{0,4},{4,0},{8,12},{12,8},{16,20},{20,16},{24,28},{28,24},{1,5},{5... | collective-permute-start | bytes 786440 | tf_op jit(solution)/shard_map/ppermute | solution.py:258
  6.0 3.0 %copy-start.16 = (bf16[4,7,128,128]{3,2,1,0:T(8,128)(2,1)S(1)}, bf16[4,7,128,128]{3,2,1,0:T(8,128)(2,1)}, u32[]{:S(2)}) copy-start(bf16[4,7,128,128]{3,2,1,0:T(8,128)(2,1)} %pack_twin.2) | copy-start | bytes 2752516
  6.0 0.7 copy-start.17
  9.0 5.9 %collective-permute-start.1 = (bf16[4,7,128,128]{3,2,1,0:T(8,128)(2,1)S(1)}, bf16[4,7,128,128]{3,2,1,0:T(8,128)(2,1)S(1)}, u32[]{:S(2)}, u32[]{:S(2)}) collective-permute-start(bf16[4,7,128,128]{3,2,1,0:T(8,128)(2,1)S(1)} %copy-done.16), channel_id=1, source_target_pairs={{0,4},{4,0},{8,12},{12,8},{16,20},{20,16},{24,28},{28,24},{1,5},{5... | collective-permute-start | bytes 2752520 | tf_op jit(solution)/shard_map/ppermute | solution.py:258
  9.2 9.9 %collective-permute-start.2 = (bf16[2,2,128,128]{3,2,1,0:T(8,128)(2,1)}, bf16[2,2,128,128]{3,2,1,0:T(8,128)(2,1)S(1)}, u32[]{:S(2)}, u32[]{:S(2)}) collective-permute-start(bf16[2,2,128,128]{3,2,1,0:T(8,128)(2,1)} %get-tuple-element.66), channel_id=1, source_target_pairs={{0,1},{1,0},{2,3},{3,2},{4,5},{5,4},{6,7},{7,6},{8,9},{9,8},{10,11... | collective-permute-start | bytes 393224 | tf_op jit(solution)/shard_map/ppermute | solution.py:255
  12.2 13.1 %collective-permute-start.4 = (bf16[2,2,128,128]{3,2,1,0:T(8,128)(2,1)}, bf16[2,2,128,128]{3,2,1,0:T(8,128)(2,1)S(1)}, u32[]{:S(2)}, u32[]{:S(2)}) collective-permute-start(bf16[2,2,128,128]{3,2,1,0:T(8,128)(2,1)} %get-tuple-element.69), channel_id=1, source_target_pairs={{0,2},{1,3},{2,0},{3,1},{4,6},{5,7},{6,4},{7,5},{8,10},{9,11},{10,... | collective-permute-start | bytes 393224 | tf_op jit(solution)/shard_map/ppermute | solution.py:255
  14.8 10.5 %collective-permute-start.6 = (bf16[2,2,128,128]{3,2,1,0:T(8,128)(2,1)}, bf16[2,2,128,128]{3,2,1,0:T(8,128)(2,1)S(1)}, u32[]{:S(2)}, u32[]{:S(2)}) collective-permute-start(bf16[2,2,128,128]{3,2,1,0:T(8,128)(2,1)} %get-tuple-element.72), channel_id=1, source_target_pairs={{0,3},{1,2},{2,1},{3,0},{4,7},{5,6},{6,5},{7,4},{8,11},{9,10},{10,... | collective-permute-start | bytes 393224 | tf_op jit(solution)/shard_map/ppermute | solution.py:255
  14.9 10.5 %copy-start.25 = (bf16[2,2,128,128]{3,2,1,0:T(8,128)(2,1)S(1)}, bf16[2,2,128,128]{3,2,1,0:T(8,128)(2,1)}, u32[]{:S(2)}) copy-start(bf16[2,2,128,128]{3,2,1,0:T(8,128)(2,1)} %get-tuple-element.74) | copy-start | bytes 393220
  14.9 1.0 copy-start.15
  25.4 3.4 %copy-start.33 = (bf16[2,3,128,128]{3,2,1,0:T(8,128)(2,1)S(1)}, bf16[2,3,128,128]{3,2,1,0:T(8,128)(2,1)}, u32[]{:S(2)}) copy-start(bf16[2,3,128,128]{3,2,1,0:T(8,128)(2,1)} %get-tuple-element.73) | copy-start | bytes 589828
  25.4 5.9 %copy-start.31 = (bf16[2,3,128,128]{3,2,1,0:T(8,128)(2,1)S(1)}, bf16[2,3,128,128]{3,2,1,0:T(8,128)(2,1)}, u32[]{:S(2)}) copy-start(bf16[2,3,128,128]{3,2,1,0:T(8,128)(2,1)} %get-tuple-element.67) | copy-start | bytes 589828
  25.4 7.3 %copy-start.32 = (bf16[2,3,128,128]{3,2,1,0:T(8,128)(2,1)S(1)}, bf16[2,3,128,128]{3,2,1,0:T(8,128)(2,1)}, u32[]{:S(2)}) copy-start(bf16[2,3,128,128]{3,2,1,0:T(8,128)(2,1)} %get-tuple-element.70) | copy-start | bytes 589828
  25.5 13.0 %collective-permute-start.8 = (bf16[4,2,2,128,128]{4,3,2,1,0:T(8,128)(2,1)S(1)}, bf16[4,2,2,128,128]{4,3,2,1,0:T(8,128)(2,1)S(1)}, u32[]{:S(2)}, u32[]{:S(2)}) collective-permute-start(bf16[4,2,2,128,128]{4,3,2,1,0:T(8,128)(2,1)S(1)} %get-tuple-element.123), channel_id=1, source_target_pairs={{0,8},{4,20},{8,0},{12,28},{16,24},{20,4},{24,16},{28,12},{1,9},{5... | collective-permute-start | bytes 1572872 | tf_op jit(solution)/shard_map/ppermute | solution.py:258
  27.1 11.5 %collective-permute-start.9 = (bf16[4,2,2,128,128]{4,3,2,1,0:T(8,128)(2,1)S(1)}, bf16[4,2,2,128,128]{4,3,2,1,0:T(8,128)(2,1)S(1)}, u32[]{:S(2)}, u32[]{:S(2)}) collective-permute-start(bf16[4,2,2,128,128]{4,3,2,1,0:T(8,128)(2,1)S(1)} %get-tuple-element.123), channel_id=1, source_target_pairs={{0,16},{4,12},{8,24},{12,4},{16,0},{20,28},{24,8},{28,20},{1,17},{... | collective-permute-start | bytes 1572872 | tf_op jit(solution)/shard_map/ppermute | solution.py:258
  28.7 9.7 %collective-permute-start.7 = (bf16[2,3,128,128]{3,2,1,0:T(8,128)(2,1)S(1)}, bf16[2,3,128,128]{3,2,1,0:T(8,128)(2,1)S(1)}, u32[]{:S(2)}, u32[]{:S(2)}) collective-permute-start(bf16[2,3,128,128]{3,2,1,0:T(8,128)(2,1)S(1)} %copy-done.33), channel_id=1, source_target_pairs={{0,3},{1,2},{2,1},{3,0},{4,7},{5,6},{6,5},{7,4},{8,11},{9,10},{10,... | collective-permute-start | bytes 589832 | tf_op jit(solution)/shard_map/ppermute | solution.py:255
  31.3 15.9 %collective-permute-start.3 = (bf16[2,3,128,128]{3,2,1,0:T(8,128)(2,1)S(1)}, bf16[2,3,128,128]{3,2,1,0:T(8,128)(2,1)S(1)}, u32[]{:S(2)}, u32[]{:S(2)}) collective-permute-start(bf16[2,3,128,128]{3,2,1,0:T(8,128)(2,1)S(1)} %copy-done.31), channel_id=1, source_target_pairs={{0,1},{1,0},{2,3},{3,2},{4,5},{5,4},{6,7},{7,6},{8,9},{9,8},{10,11... | collective-permute-start | bytes 589832 | tf_op jit(solution)/shard_map/ppermute | solution.py:255
  32.7 14.5 %collective-permute-start.5 = (bf16[2,3,128,128]{3,2,1,0:T(8,128)(2,1)S(1)}, bf16[2,3,128,128]{3,2,1,0:T(8,128)(2,1)S(1)}, u32[]{:S(2)}, u32[]{:S(2)}) collective-permute-start(bf16[2,3,128,128]{3,2,1,0:T(8,128)(2,1)S(1)} %copy-done.32), channel_id=1, source_target_pairs={{0,2},{1,3},{2,0},{3,1},{4,6},{5,7},{6,4},{7,5},{8,10},{9,11},{10,... | collective-permute-start | bytes 589832 | tf_op jit(solution)/shard_map/ppermute | solution.py:255
  38.6 8.7 %collective-permute-start.10 = (bf16[2,2,2,128,128]{4,3,2,1,0:T(8,128)(2,1)S(1)}, bf16[2,2,2,128,128]{4,3,2,1,0:T(8,128)(2,1)S(1)}, u32[]{:S(2)}, u32[]{:S(2)}) collective-permute-start(bf16[2,2,2,128,128]{4,3,2,1,0:T(8,128)(2,1)S(1)} %slice.104), channel_id=1, source_target_pairs={{0,16},{4,12},{8,24},{12,4},{16,0},{20,28},{24,8},{28,20},{1,17},{... | collective-permute-start | bytes 786440 | tf_op jit(solution)/shard_map/ppermute | solution.py:258
  39.2 8.1 %collective-permute-start.11 = (bf16[2,2,2,128,128]{4,3,2,1,0:T(8,128)(2,1)S(1)}, bf16[2,2,2,128,128]{4,3,2,1,0:T(8,128)(2,1)S(1)}, u32[]{:S(2)}, u32[]{:S(2)}) collective-permute-start(bf16[2,2,2,128,128]{4,3,2,1,0:T(8,128)(2,1)S(1)} %slice.105), channel_id=1, source_target_pairs={{0,8},{4,20},{8,0},{12,28},{16,24},{20,4},{24,16},{28,12},{1,9},{5... | collective-permute-start | bytes 786440 | tf_op jit(solution)/shard_map/ppermute | solution.py:258
  47.2 0.9 copy-start.7
  48.2 1.4 %copy-start.30 = (bf16[2,3,128,128]{3,2,1,0:T(8,128)(2,1)S(1)}, bf16[2,3,128,128]{3,2,1,0:T(8,128)(2,1)}, u32[]{:S(2)}) copy-start(bf16[2,3,128,128]{3,2,1,0:T(8,128)(2,1)} %get-tuple-element.99) | copy-start | bytes 589828
  48.2 3.8 %copy-start.29 = (bf16[2,3,128,128]{3,2,1,0:T(8,128)(2,1)S(1)}, bf16[2,3,128,128]{3,2,1,0:T(8,128)(2,1)}, u32[]{:S(2)}) copy-start(bf16[2,3,128,128]{3,2,1,0:T(8,128)(2,1)} %get-tuple-element.96) | copy-start | bytes 589828
  48.2 9.1 %copy-start.28 = (bf16[2,3,128,128]{3,2,1,0:T(8,128)(2,1)S(1)}, bf16[2,3,128,128]{3,2,1,0:T(8,128)(2,1)}, u32[]{:S(2)}) copy-start(bf16[2,3,128,128]{3,2,1,0:T(8,128)(2,1)} %get-tuple-element.93) | copy-start | bytes 589828
  48.2 9.1 %copy-start.9 = (s32[6,32,32]{2,1,0:T(8,128)S(1)}, s32[6,32,32]{2,1,0:T(8,128)}, u32[]{:S(2)}) copy-start(s32[6,32,32]{2,1,0:T(8,128)} %mask_ref.5) | copy-start | bytes 73732
  48.2 9.1 %copy-start.10 = (bf16[2,1,128,128]{3,2,1,0:T(8,128)(2,1)S(1)}, bf16[2,1,128,128]{3,2,1,0:T(8,128)(2,1)}, u32[]{:S(2)}) copy-start(bf16[2,1,128,128]{3,2,1,0:T(8,128)(2,1)} %get-tuple-element.79.refs_9_) | copy-start | bytes 196612
  48.2 9.1 %copy-start.11 = (bf16[2,1,128,128]{3,2,1,0:T(8,128)(2,1)S(1)}, bf16[2,1,128,128]{3,2,1,0:T(8,128)(2,1)}, u32[]{:S(2)}) copy-start(bf16[2,1,128,128]{3,2,1,0:T(8,128)(2,1)} %get-tuple-element.80.refs_10_) | copy-start | bytes 196612
  48.2 9.1 %copy-start.12 = (bf16[2,1,128,128]{3,2,1,0:T(8,128)(2,1)S(1)}, bf16[2,1,128,128]{3,2,1,0:T(8,128)(2,1)}, u32[]{:S(2)}) copy-start(bf16[2,1,128,128]{3,2,1,0:T(8,128)(2,1)} %get-tuple-element.81.refs_11_) | copy-start | bytes 196612
  48.2 9.1 %copy-start.13 = (bf16[2,1,128,128]{3,2,1,0:T(8,128)(2,1)S(1)}, bf16[2,1,128,128]{3,2,1,0:T(8,128)(2,1)}, u32[]{:S(2)}) copy-start(bf16[2,1,128,128]{3,2,1,0:T(8,128)(2,1)} %get-tuple-element.82.refs_12_) | copy-start | bytes 196612
  48.4 19.0 %collective-permute-start.12 = (bf16[4,2,2,128,128]{4,3,2,1,0:T(8,128)(2,1)S(1)}, bf16[4,2,2,128,128]{4,3,2,1,0:T(8,128)(2,1)S(1)}, u32[]{:S(2)}, u32[]{:S(2)}) collective-permute-start(bf16[4,2,2,128,128]{4,3,2,1,0:T(8,128)(2,1)S(1)} %get-tuple-element.122), channel_id=1, source_target_pairs={{0,8},{4,20},{8,0},{12,28},{16,24},{20,4},{24,16},{28,12},{1,9},{5... | collective-permute-start | bytes 1572872 | tf_op jit(solution)/shard_map/ppermute | solution.py:258
  49.0 18.4 %collective-permute-start.13 = (bf16[4,2,2,128,128]{4,3,2,1,0:T(8,128)(2,1)S(1)}, bf16[4,2,2,128,128]{4,3,2,1,0:T(8,128)(2,1)S(1)}, u32[]{:S(2)}, u32[]{:S(2)}) collective-permute-start(bf16[4,2,2,128,128]{4,3,2,1,0:T(8,128)(2,1)S(1)} %get-tuple-element.122), channel_id=1, source_target_pairs={{0,16},{4,12},{8,24},{12,4},{16,0},{20,28},{24,8},{28,20},{1,17},{... | collective-permute-start | bytes 1572872 | tf_op jit(solution)/shard_map/ppermute | solution.py:258
  49.6 17.7 %collective-permute-start.18 = (bf16[2,3,128,128]{3,2,1,0:T(8,128)(2,1)S(1)}, bf16[2,3,128,128]{3,2,1,0:T(8,128)(2,1)S(1)}, u32[]{:S(2)}, u32[]{:S(2)}) collective-permute-start(bf16[2,3,128,128]{3,2,1,0:T(8,128)(2,1)S(1)} %copy-done.30), channel_id=1, source_target_pairs={{0,3},{1,2},{2,1},{3,0},{4,7},{5,6},{6,5},{7,4},{8,11},{9,10},{10,... | collective-permute-start | bytes 589832 | tf_op jit(solution)/shard_map/ppermute | solution.py:255
  52.0 17.6 %collective-permute-start.17 = (bf16[2,3,128,128]{3,2,1,0:T(8,128)(2,1)S(1)}, bf16[2,3,128,128]{3,2,1,0:T(8,128)(2,1)S(1)}, u32[]{:S(2)}, u32[]{:S(2)}) collective-permute-start(bf16[2,3,128,128]{3,2,1,0:T(8,128)(2,1)S(1)} %copy-done.29), channel_id=1, source_target_pairs={{0,2},{1,3},{2,0},{3,1},{4,6},{5,7},{6,4},{7,5},{8,10},{9,11},{10,... | collective-permute-start | bytes 589832 | tf_op jit(solution)/shard_map/ppermute | solution.py:255
  57.3 12.4 %collective-permute-start.16 = (bf16[2,3,128,128]{3,2,1,0:T(8,128)(2,1)S(1)}, bf16[2,3,128,128]{3,2,1,0:T(8,128)(2,1)S(1)}, u32[]{:S(2)}, u32[]{:S(2)}) collective-permute-start(bf16[2,3,128,128]{3,2,1,0:T(8,128)(2,1)S(1)} %copy-done.28), channel_id=1, source_target_pairs={{0,1},{1,0},{2,3},{3,2},{4,5},{5,4},{6,7},{7,6},{8,9},{9,8},{10,11... | collective-permute-start | bytes 589832 | tf_op jit(solution)/shard_map/ppermute | solution.py:255
  57.3 0.7 copy-start.14
  67.3 41.2 %copy-start = (bf16[2,2,128,128]{3,2,1,0:T(8,128)(2,1)}, bf16[2,2,128,128]{3,2,1,0:T(8,128)(2,1)S(1)}, u32[]{:S(2)}) copy-start(bf16[2,2,128,128]{3,2,1,0:T(8,128)(2,1)S(1)} %get-tuple-element.100.refs_0_) | copy-start | bytes 393220
  67.4 9.2 %collective-permute-start.14 = (bf16[2,2,2,128,128]{4,3,2,1,0:T(8,128)(2,1)S(1)}, bf16[2,2,2,128,128]{4,3,2,1,0:T(8,128)(2,1)S(1)}, u32[]{:S(2)}, u32[]{:S(2)}) collective-permute-start(bf16[2,2,2,128,128]{4,3,2,1,0:T(8,128)(2,1)S(1)} %slice.109), channel_id=1, source_target_pairs={{0,16},{4,12},{8,24},{12,4},{16,0},{20,28},{24,8},{28,20},{1,17},{... | collective-permute-start | bytes 786440 | tf_op jit(solution)/shard_map/ppermute | solution.py:258
  68.1 9.2 %collective-permute-start.15 = (bf16[2,2,2,128,128]{4,3,2,1,0:T(8,128)(2,1)S(1)}, bf16[2,2,2,128,128]{4,3,2,1,0:T(8,128)(2,1)S(1)}, u32[]{:S(2)}, u32[]{:S(2)}) collective-permute-start(bf16[2,2,2,128,128]{4,3,2,1,0:T(8,128)(2,1)S(1)} %slice.110), channel_id=1, source_target_pairs={{0,8},{4,20},{8,0},{12,28},{16,24},{20,4},{24,16},{28,12},{1,9},{5... | collective-permute-start | bytes 786440 | tf_op jit(solution)/shard_map/ppermute | solution.py:258
  69.7 7.7 %copy-start.6 = (bf16[2,3,128,128]{3,2,1,0:T(8,128)(2,1)S(1)}, bf16[2,3,128,128]{3,2,1,0:T(8,128)(2,1)}, u32[]{:S(2)}) copy-start(bf16[2,3,128,128]{3,2,1,0:T(8,128)(2,1)} %get-tuple-element.90.refs_0_) | copy-start | bytes 589828
  77.4 16.6 %collective-permute-start.22 = (bf16[4,2,2,128,128]{4,3,2,1,0:T(8,128)(2,1)S(1)}, bf16[4,2,2,128,128]{4,3,2,1,0:T(8,128)(2,1)S(1)}, u32[]{:S(2)}, u32[]{:S(2)}) collective-permute-start(bf16[4,2,2,128,128]{4,3,2,1,0:T(8,128)(2,1)S(1)} %get-tuple-element.120), channel_id=1, source_target_pairs={{0,8},{4,20},{8,0},{12,28},{16,24},{20,4},{24,16},{28,12},{1,9},{5... | collective-permute-start | bytes 1572872 | tf_op jit(solution)/shard_map/ppermute | solution.py:258
  79.0 15.1 %collective-permute-start.23 = (bf16[4,2,2,128,128]{4,3,2,1,0:T(8,128)(2,1)S(1)}, bf16[4,2,2,128,128]{4,3,2,1,0:T(8,128)(2,1)S(1)}, u32[]{:S(2)}, u32[]{:S(2)}) collective-permute-start(bf16[4,2,2,128,128]{4,3,2,1,0:T(8,128)(2,1)S(1)} %get-tuple-element.120), channel_id=1, source_target_pairs={{0,16},{4,12},{8,24},{12,4},{16,0},{20,28},{24,8},{28,20},{1,17},{... | collective-permute-start | bytes 1572872 | tf_op jit(solution)/shard_map/ppermute | solution.py:258
  80.4 13.5 %collective-permute-start.19 = (bf16[2,2,128,128]{3,2,1,0:T(8,128)(2,1)S(1)}, bf16[2,2,128,128]{3,2,1,0:T(8,128)(2,1)S(1)}, u32[]{:S(2)}, u32[]{:S(2)}) collective-permute-start(bf16[2,2,128,128]{3,2,1,0:T(8,128)(2,1)S(1)} %get-tuple-element.101), channel_id=1, source_target_pairs={{0,1},{1,0},{2,3},{3,2},{4,5},{5,4},{6,7},{7,6},{8,9},{9,8},{10,11... | collective-permute-start | bytes 393224 | tf_op jit(solution)/shard_map/ppermute | solution.py:255
  82.0 11.8 %collective-permute-start.20 = (bf16[2,2,128,128]{3,2,1,0:T(8,128)(2,1)S(1)}, bf16[2,2,128,128]{3,2,1,0:T(8,128)(2,1)S(1)}, u32[]{:S(2)}, u32[]{:S(2)}) collective-permute-start(bf16[2,2,128,128]{3,2,1,0:T(8,128)(2,1)S(1)} %get-tuple-element.102), channel_id=1, source_target_pairs={{0,2},{1,3},{2,0},{3,1},{4,6},{5,7},{6,4},{7,5},{8,10},{9,11},{10,... | collective-permute-start | bytes 393224 | tf_op jit(solution)/shard_map/ppermute | solution.py:255
  83.2 10.6 %collective-permute-start.21 = (bf16[2,2,128,128]{3,2,1,0:T(8,128)(2,1)S(1)}, bf16[2,2,128,128]{3,2,1,0:T(8,128)(2,1)S(1)}, u32[]{:S(2)}, u32[]{:S(2)}) collective-permute-start(bf16[2,2,128,128]{3,2,1,0:T(8,128)(2,1)S(1)} %get-tuple-element.103), channel_id=1, source_target_pairs={{0,3},{1,2},{2,1},{3,0},{4,7},{5,6},{6,5},{7,4},{8,11},{9,10},{10,... | collective-permute-start | bytes 393224 | tf_op jit(solution)/shard_map/ppermute | solution.py:255
  93.8 5.0 %copy-start.4 = (bf16[2,1,128,128]{3,2,1,0:T(8,128)(2,1)}, bf16[2,1,128,128]{3,2,1,0:T(8,128)(2,1)S(1)}, u32[]{:S(2)}) copy-start(bf16[2,1,128,128]{3,2,1,0:T(8,128)(2,1)S(1)} %get-tuple-element.111.refs_4_) | copy-start | bytes 196612
  93.8 14.7 %copy-start.3 = (bf16[2,2,128,128]{3,2,1,0:T(8,128)(2,1)}, bf16[2,2,128,128]{3,2,1,0:T(8,128)(2,1)S(1)}, u32[]{:S(2)}) copy-start(bf16[2,2,128,128]{3,2,1,0:T(8,128)(2,1)S(1)} %collective-permute-done.21.refs_3_) | copy-start | bytes 393220
  93.9 14.6 %copy-start.2 = (bf16[2,2,128,128]{3,2,1,0:T(8,128)(2,1)}, bf16[2,2,128,128]{3,2,1,0:T(8,128)(2,1)S(1)}, u32[]{:S(2)}) copy-start(bf16[2,2,128,128]{3,2,1,0:T(8,128)(2,1)S(1)} %collective-permute-done.20.refs_2_) | copy-start | bytes 393220
  93.9 14.6 %copy-start.1 = (bf16[2,2,128,128]{3,2,1,0:T(8,128)(2,1)}, bf16[2,2,128,128]{3,2,1,0:T(8,128)(2,1)S(1)}, u32[]{:S(2)}) copy-start(bf16[2,2,128,128]{3,2,1,0:T(8,128)(2,1)S(1)} %collective-permute-done.19.refs_1_) | copy-start | bytes 393220
  94.0 34.0 %collective-permute-start.32 = (bf16[4,128,128]{2,1,0:T(8,128)(2,1)S(1)}, bf16[4,128,128]{2,1,0:T(8,128)(2,1)S(1)}, u32[]{:S(2)}, u32[]{:S(2)}) collective-permute-start(bf16[4,128,128]{2,1,0:T(8,128)(2,1)S(1)} %pad_maximum_fusion.3), channel_id=1, source_target_pairs={{0,4},{4,0},{8,12},{12,8},{16,20},{20,16},{24,28},{28,24},{1,5},{5... | collective-permute-start | bytes 393224 | tf_op jit(solution)/shard_map/ppermute | solution.py:258
  94.1 14.4 %collective-permute-start.27 = (bf16[2,2,2,128,128]{4,3,2,1,0:T(8,128)(2,1)S(1)}, bf16[2,2,2,128,128]{4,3,2,1,0:T(8,128)(2,1)S(1)}, u32[]{:S(2)}, u32[]{:S(2)}) collective-permute-start(bf16[2,2,2,128,128]{4,3,2,1,0:T(8,128)(2,1)S(1)} %slice.114), channel_id=1, source_target_pairs={{0,16},{4,12},{8,24},{12,4},{16,0},{20,28},{24,8},{28,20},{1,17},{... | collective-permute-start | bytes 786440 | tf_op jit(solution)/shard_map/ppermute | solution.py:258
  94.9 13.6 %collective-permute-start.28 = (bf16[2,2,2,128,128]{4,3,2,1,0:T(8,128)(2,1)S(1)}, bf16[2,2,2,128,128]{4,3,2,1,0:T(8,128)(2,1)S(1)}, u32[]{:S(2)}, u32[]{:S(2)}) collective-permute-start(bf16[2,2,2,128,128]{4,3,2,1,0:T(8,128)(2,1)S(1)} %slice.115), channel_id=1, source_target_pairs={{0,8},{4,20},{8,0},{12,28},{16,24},{20,4},{24,16},{28,12},{1,9},{5... | collective-permute-start | bytes 786440 | tf_op jit(solution)/shard_map/ppermute | solution.py:258
  95.4 12.4 %collective-permute-start.24 = (bf16[2,1,128,128]{3,2,1,0:T(8,128)(2,1)S(1)}, bf16[2,1,128,128]{3,2,1,0:T(8,128)(2,1)S(1)}, u32[]{:S(2)}, u32[]{:S(2)}) collective-permute-start(bf16[2,1,128,128]{3,2,1,0:T(8,128)(2,1)S(1)} %get-tuple-element.112), channel_id=1, source_target_pairs={{0,1},{1,0},{2,3},{3,2},{4,5},{5,4},{6,7},{7,6},{8,9},{9,8},{10,11... | collective-permute-start | bytes 196616 | tf_op jit(solution)/shard_map/ppermute | solution.py:255
  96.5 6.1 %collective-permute-start.26 = (bf16[2,1,128,128]{3,2,1,0:T(8,128)(2,1)S(1)}, bf16[2,1,128,128]{3,2,1,0:T(8,128)(2,1)S(1)}, u32[]{:S(2)}, u32[]{:S(2)}) collective-permute-start(bf16[2,1,128,128]{3,2,1,0:T(8,128)(2,1)S(1)} %get-tuple-element.114), channel_id=1, source_target_pairs={{0,3},{1,2},{2,1},{3,0},{4,7},{5,6},{6,5},{7,4},{8,11},{9,10},{10,... | collective-permute-start | bytes 196616 | tf_op jit(solution)/shard_map/ppermute | solution.py:255
  102.6 5.3 %copy-start.19 = (bf16[2,1,128,128]{3,2,1,0:T(8,128)(2,1)}, bf16[2,1,128,128]{3,2,1,0:T(8,128)(2,1)S(1)}, u32[]{:S(2)}) copy-start(bf16[2,1,128,128]{3,2,1,0:T(8,128)(2,1)S(1)} %collective-permute-done.26.refs_7_) | copy-start | bytes 196612
  102.6 5.2 %collective-permute-start.25 = (bf16[2,1,128,128]{3,2,1,0:T(8,128)(2,1)S(1)}, bf16[2,1,128,128]{3,2,1,0:T(8,128)(2,1)S(1)}, u32[]{:S(2)}, u32[]{:S(2)}) collective-permute-start(bf16[2,1,128,128]{3,2,1,0:T(8,128)(2,1)S(1)} %get-tuple-element.113), channel_id=1, source_target_pairs={{0,2},{1,3},{2,0},{3,1},{4,6},{5,7},{6,4},{7,5},{8,10},{9,11},{10,... | collective-permute-start | bytes 196616 | tf_op jit(solution)/shard_map/ppermute | solution.py:255
  107.8 0.7 copy-start.18
  108.5 19.5 %collective-permute-start.33 = (bf16[4,128,128]{2,1,0:T(8,128)(2,1)S(1)}, bf16[4,128,128]{2,1,0:T(8,128)(2,1)S(1)}, u32[]{:S(2)}, u32[]{:S(2)}) collective-permute-start(bf16[4,128,128]{2,1,0:T(8,128)(2,1)S(1)} %pad_maximum_fusion.4), channel_id=1, source_target_pairs={{0,4},{4,0},{8,12},{12,8},{16,20},{20,16},{24,28},{28,24},{1,5},{5... | collective-permute-start | bytes 393224 | tf_op jit(solution)/shard_map/ppermute | solution.py:258
  117.8 9.0 %copy-start.5 = (bf16[2,1,128,128]{3,2,1,0:T(8,128)(2,1)}, bf16[2,1,128,128]{3,2,1,0:T(8,128)(2,1)S(1)}, u32[]{:S(2)}) copy-start(bf16[2,1,128,128]{3,2,1,0:T(8,128)(2,1)S(1)} %get-tuple-element.115.refs_8_) | copy-start | bytes 196612
  117.8 9.6 %collective-permute-start.29 = (bf16[2,1,128,128]{3,2,1,0:T(8,128)(2,1)S(1)}, bf16[2,1,128,128]{3,2,1,0:T(8,128)(2,1)S(1)}, u32[]{:S(2)}, u32[]{:S(2)}) collective-permute-start(bf16[2,1,128,128]{3,2,1,0:T(8,128)(2,1)S(1)} %get-tuple-element.116), channel_id=1, source_target_pairs={{0,1},{1,0},{2,3},{3,2},{4,5},{5,4},{6,7},{7,6},{8,9},{9,8},{10,11... | collective-permute-start | bytes 196616 | tf_op jit(solution)/shard_map/ppermute | solution.py:255
  117.8 8.9 %collective-permute-start.30 = (bf16[2,1,128,128]{3,2,1,0:T(8,128)(2,1)S(1)}, bf16[2,1,128,128]{3,2,1,0:T(8,128)(2,1)S(1)}, u32[]{:S(2)}, u32[]{:S(2)}) collective-permute-start(bf16[2,1,128,128]{3,2,1,0:T(8,128)(2,1)S(1)} %get-tuple-element.117), channel_id=1, source_target_pairs={{0,2},{1,3},{2,0},{3,1},{4,6},{5,7},{6,4},{7,5},{8,10},{9,11},{10,... | collective-permute-start | bytes 196616 | tf_op jit(solution)/shard_map/ppermute | solution.py:255
  120.6 6.1 %collective-permute-start.31 = (bf16[2,1,128,128]{3,2,1,0:T(8,128)(2,1)S(1)}, bf16[2,1,128,128]{3,2,1,0:T(8,128)(2,1)S(1)}, u32[]{:S(2)}, u32[]{:S(2)}) collective-permute-start(bf16[2,1,128,128]{3,2,1,0:T(8,128)(2,1)S(1)} %get-tuple-element.118), channel_id=1, source_target_pairs={{0,3},{1,2},{2,1},{3,0},{4,7},{5,6},{6,5},{7,4},{8,11},{9,10},{10,... | collective-permute-start | bytes 196616 | tf_op jit(solution)/shard_map/ppermute | solution.py:255
  128.0 1.3 %collective-permute-start.34 = (bf16[4,128,128]{2,1,0:T(8,128)(2,1)S(1)}, bf16[4,128,128]{2,1,0:T(8,128)(2,1)S(1)}, u32[]{:S(2)}, u32[]{:S(2)}) collective-permute-start(bf16[4,128,128]{2,1,0:T(8,128)(2,1)S(1)} %pad_maximum_fusion.5), channel_id=1, source_target_pairs={{0,4},{4,0},{8,12},{12,8},{16,20},{20,16},{24,28},{28,24},{1,5},{5... | collective-permute-start | bytes 393224 | tf_op jit(solution)/shard_map/ppermute | solution.py:258
  128.0 1.3 %copy-start.24 = (bf16[4,128,128]{2,1,0:T(8,128)(2,1)}, bf16[4,128,128]{2,1,0:T(8,128)(2,1)S(1)}, u32[]{:S(2)}) copy-start(bf16[4,128,128]{2,1,0:T(8,128)(2,1)S(1)} %collective-permute-done.32.refs_12_) | copy-start | bytes 393220
  128.0 1.3 %copy-start.26 = (bf16[4,128,128]{2,1,0:T(8,128)(2,1)}, bf16[4,128,128]{2,1,0:T(8,128)(2,1)S(1)}, u32[]{:S(2)}) copy-start(bf16[4,128,128]{2,1,0:T(8,128)(2,1)S(1)} %collective-permute-done.33.refs_13_) | copy-start | bytes 393220
  129.3 0.7 copy-start.27
  (5 other events, 3.1 us)
where the time goes:
time: 133 us; the launch traced here: 132 us
  starting transfers between devices  44.2 us (33%)
  Pallas kernels  40.5 us (30%)
  waiting for transfers between devices  39.7 us (30%)
  local copies, waits for them, and re-layouts  6.24 us (5%)
    ppermute x18, waiting for transfers between devices, swap(): return lax.ppermute(array, 'head', [(z, z ^ way) for z in range(ways)])  30.8 us
    ppermute x18, starting transfers between devices, swap(): return lax.ppermute(array, 'head', [(z, z ^ way) for z in range(ways)])  30.7 us
    pallas_call x3, Pallas kernels, attend(): pl.pallas_call(body, grid_spec=pltpu.PrefetchScalarGridSpec(num_scalar_pr...  27.6 us
    ppermute x17, starting transfers between devices, send(): return lax.ppermute(array, 'seq', pairs)  13.5 us
    pallas_call x5, Pallas kernels, in_vmem(): pl.pallas_call(body, in_specs=[pl.BlockSpec(memory_space=pltpu.SMEM)] + [...  13 us
    ppermute x17, waiting for transfers between devices, send(): return lax.ppermute(array, 'seq', pairs)  8.97 us
    unnamed x68, local copies, waits for them, and re-layouts  5.66 us
  transfers between devices with their start and end apart: 35, of which 9 were waited for; matrix products, arithmetic and copies ran while one was open for 1% of the time, Pallas kernels for 25%

commit v1 on v0

--- a/solution.py
+++ b/solution.py
@@ -90,12 +90,15 @@
     return in_vmem(body, out, "unpack", place, *operands)
 
 
-def attend(place, layout, query_ids, key_ids, block_mask, turn, queries, parts, extra, shape):
+def attend(
+    place, layout, query_ids, key_ids, block_mask, turn, queries, parts, extra, shape, state, first_block, last
+):
     cores, turns = shape
     ways, rows = len(queries), queries[0].shape[2]
     query_part = queries[0].shape[1] - 1
     units = ways * cores * rows // BLOCK
     blocks = sum(part.shape[0] * part.shape[1] for part in parts) * cores * rows // BLOCK
+    mask_blocks = layout.shape[0]
     width = blocks * BLOCK
     group = max(1, min(units, SCORE_BYTES // (4 * BLOCK * width)))
     while units % group:
@@ -110,7 +113,9 @@
 
     def body(place_ref, layout_ref, query_ids_ref, key_ids_ref, mask_ref, *refs):
         query_refs, part_refs = refs[:ways], refs[ways : ways + len(parts)]
-        extra_refs, out_refs = refs[ways + len(parts) : -3 - ways], refs[-3 - ways : -3]
+        state_refs = refs[ways + len(parts) :][: len(state)]
+        extra_refs = refs[ways + len(parts) + len(state) :][: len(extra)]
+        out_refs = refs[ways + len(parts) + len(state) + len(extra) : -3]
         scores, asked, answered = refs[-3:]
         for way in range(ways):
             for other in range(cores):
@@ -124,7 +129,10 @@
         def step(lot, carry):
             tile = asked[pl.ds(pl.multiple_of(lot * group * BLOCK, BLOCK), group * BLOCK)]
             mask_rows = [layout_ref[query_ids_ref[lot * group + at]] for at in range(group)]
-            maxima = [None] * group
+            spots = [
+                pl.ds(pl.multiple_of((lot * group + at) * BLOCK, BLOCK), BLOCK) for at in range(group)
+            ]
+            maxima = [state_refs[0][spot] if state else None for spot in spots]
             block = 0
             for lot_at in lots:
                 found = lax.dot_general(
@@ -134,7 +142,7 @@
                     preferred_element_type=jnp.float32,
                 )
                 for unit in range(lot_at[-1]):
-                    column = layout_ref[key_ids_ref[block]]
+                    column = layout_ref[key_ids_ref[first_block + block]]
                     for at in range(group):
                         allowed = mask_ref[0, mask_rows[at], column] > 0
                         bias = jnp.where(allowed, jnp.float32(0), jnp.float32(-jnp.inf))
@@ -150,8 +158,13 @@
                         maxima[at] = piece if maxima[at] is None else jnp.maximum(maxima[at], piece)
                     block += 1
             for at in range(group):
-                shift = jnp.max(maxima[at], axis=1, keepdims=True) * EXP2_SCALE
+                peak = jnp.max(maxima[at], axis=1, keepdims=True)
+                shift = peak * EXP2_SCALE
                 total = accum = None
+                if state:
+                    factor = jnp.exp2(state_refs[0][spots[at]] * EXP2_SCALE - shift)
+                    total = state_refs[1][spots[at]] * factor
+                    accum = state_refs[2][spots[at]] * factor
                 block = 0
                 for lot_at in lots:
                     count = lot_at[-1]
@@ -169,19 +182,29 @@
                     )
                     accum = product if accum is None else accum + product
                     block += count
-                total = jnp.sum(total, axis=1, keepdims=True)
-                spot = pl.multiple_of((lot * group + at) * BLOCK, BLOCK)
-                answered[pl.ds(spot, BLOCK)] = (accum / total).astype(jnp.bfloat16)
+                if last:
+                    total = jnp.sum(total, axis=1, keepdims=True)
+                    answered[spots[at]] = (accum / total).astype(jnp.bfloat16)
+                else:
+                    out_refs[0][spots[at]] = jnp.broadcast_to(peak, (BLOCK, HEAD_DIM))
+                    out_refs[1][spots[at]] = total
+                    out_refs[2][spots[at]] = accum
             return carry
 
         lax.fori_loop(0, units // group, step, 0)
-        for way in range(ways):
+        for way in range(ways if last else 0):
             for other in range(cores):
                 at = (way * cores + other) * rows
                 out_refs[way][other, 0] = answered[at : at + rows]
                 if extra:
                     out_refs[way][other, 1] = extra_refs[way][other, 0]
 
+    if last:
+        out_shape = [
+            jax.ShapeDtypeStruct((cores, 2 if extra else 1, rows, HEAD_DIM), jnp.bfloat16)
+        ] * ways
+    else:
+        out_shape = [jax.ShapeDtypeStruct((units * BLOCK, HEAD_DIM), jnp.float32)] * 3
     whole = pl.BlockSpec(memory_space=pltpu.VMEM)
     return pl.pallas_call(
         body,
@@ -190,23 +213,20 @@
             grid=(1,),
             in_specs=[
                 pl.BlockSpec(
-                    (1, blocks, blocks),
+                    (1, mask_blocks, mask_blocks),
                     lambda step, place, *_: (place[0] * turns + turn, 0, 0),
                     memory_space=pltpu.SMEM,
                 )
             ]
-            + [whole] * (ways + len(parts) + len(extra)),
-            out_specs=[whole] * ways,
+            + [whole] * (ways + len(parts) + len(state) + len(extra)),
+            out_specs=[whole] * len(out_shape),
             scratch_shapes=[
                 pltpu.VMEM((group * BLOCK, width), jnp.float32),
                 pltpu.VMEM((units * BLOCK, HEAD_DIM), jnp.bfloat16),
                 pltpu.VMEM((units * BLOCK, HEAD_DIM), jnp.bfloat16),
             ],
         ),
-        out_shape=[
-            jax.ShapeDtypeStruct((cores, 2 if extra else 1, rows, HEAD_DIM), jnp.bfloat16)
-        ]
-        * ways,
+        out_shape=out_shape,
         compiler_params=pltpu.CompilerParams(vmem_limit_bytes=KERNEL_VMEM),
         cost_estimate=pl.CostEstimate(
             flops=40 * units * BLOCK * width * HEAD_DIM,
@@ -214,7 +234,7 @@
             transcendentals=units * BLOCK * width,
         ),
         name="attend",
-    )(place, layout, query_ids, key_ids, block_mask, *queries, *parts, *extra)
+    )(place, layout, query_ids, key_ids, block_mask, *queries, *parts, *state, *extra)
 
 
 def after(array, *others):
@@ -314,8 +334,6 @@
             result = lax.optimization_barrier((*result, *sidelong))[: len(result)]
         result = [result[0]] + [swap(result[way], way) for way in range(1, ways)]
         returned.append(result)
-        if relay:
-            back.append(send(jnp.stack([piece[1, 0] for piece in result]), twins))
 
     sidelong = []
     exchange(0)
@@ -333,17 +351,21 @@
             parts[0] = after(parts[0], shared[turn + 1])
         asked = held[turn + 1] if turn + 1 < turns else returned[0]
         extra = sent[turns] if turn == 0 else []
-        outs.append(
-            attend(
-                place, layout, query_ids, key_ids, block_mask, turn, asked, parts, extra, shape
-            )
-        )
+        fixed = (place, layout, query_ids, key_ids, block_mask, turn, asked)
+        state, first_block = [], 0
+        if relay and turn + 1 == turns:
+            state = attend(*fixed, parts[:3], [], shape, [], 0, False)
+            first_block, parts = 3 * ways * cores, parts[3:]
+        outs.append(attend(*fixed, parts, extra, shape, state, first_block, True))
         if turn and turn + 1 < turns:
             bring_back(turn - 1)
         if turn + 1 < turns:
             pieces.append(onward(outs[turn]) if relay else onward)
     for turn in range(len(returned), turns):
         bring_back(turn)
+    for result in returned if relay else []:
+        joined = jnp.stack([piece[1, 0] for piece in result])
+        back.append(send(after(joined, outs[-1][0]), twins))
     return unpack(place, returned, back, shape)
 
 

time: 133 us -> 127 us (0.955)
  waiting for transfers between devices: 39.7 us -> 30.9 us
    ppermute x18, waiting for transfers between devices: 30.8 us -> 21.9 us  [swap(): return lax.ppermute(array, 'head', [(z, z ^ way) for z in range(ways)])]
    pallas_call x3 -> x4, Pallas kernels: 27.6 us -> 28.7 us  [attend(): pl.pallas_call(body, grid_spec=pltpu.PrefetchScalarGridSpec(num_scalar_pr...]
  transfers between devices with their start and end apart: 35 -> 35, of which waited for: 9 -> 7; matrix products, arithmetic and copies ran while one was open for 1% -> 1% of each run, Pallas kernels for 25% -> 25%
where the time goes in v1:
time: 127 us; the launch traced here: 126 us
  starting transfers between devices  44.9 us (35%)
  Pallas kernels  41.7 us (33%)
  waiting for transfers between devices  30.9 us (24%)
  local copies, waits for them, and re-layouts  6.86 us (5%)
    ppermute x18, starting transfers between devices, swap(): return lax.ppermute(array, 'head', [(z, z ^ way) for z in range(ways)])  31 us
    pallas_call x4, Pallas kernels, attend(): pl.pallas_call(body, grid_spec=pltpu.PrefetchScalarGridSpec(num_scalar_pr...  28.7 us
    ppermute x18, waiting for transfers between devices, swap(): return lax.ppermute(array, 'head', [(z, z ^ way) for z in range(ways)])  21.9 us
    ppermute x17, starting transfers between devices, send(): return lax.ppermute(array, 'seq', pairs)  13.9 us
    pallas_call x5, Pallas kernels, in_vmem(): pl.pallas_call(body, in_specs=[pl.BlockSpec(memory_space=pltpu.SMEM)] + [...  13 us
    ppermute x17, waiting for transfers between devices, send(): return lax.ppermute(array, 'seq', pairs)  8.98 us
    unnamed x68, local copies, waits for them, and re-layouts  6.28 us
  transfers between devices with their start and end apart: 35, of which 7 were waited for; matrix products, arithmetic and copies ran while one was open for 1% of the time, Pallas kernels for 25%

profile of v1, /device:TPU:0, one launch (start us, length us, event | category | flops | bytes accessed | tf_op | source)
XLA Modules:
  0.0 126.3 jit_solution(18135169164970366574)
XLA Ops:
  0.0 0.6 pad_add_fusion.place_ref
  0.6 2.2 %pack_twin.3 = bf16[4,2,128,128]{3,2,1,0:T(8,128)(2,1)} custom-call(s32[2]{0:T(128)} %pad_add_fusion.place_ref, bf16[128,3072]{1,0:T(8,128)(2,1)} %refs_0_.7, bf16[128,3072]{1,0:T(8,128)(2,1)} %refs_1_.7), custom_call_target="tpu_custom_call" | custom-call | tf_op jit(solution)/shard_map/pack_twin/pallas_call | solution.py:25
  2.8 0.5 collective-permute-start
  3.3 2.8 %pack_twin.2 = bf16[4,7,128,128]{3,2,1,0:T(8,128)(2,1)} custom-call(s32[2]{0:T(128)} %pad_add_fusion.place_ref, bf16[128,3072]{1,0:T(8,128)(2,1)} %refs_0_.7, bf16[128,3072]{1,0:T(8,128)(2,1)} %refs_1_.7, bf16[128,3072]{1,0:T(8,128)(2,1)} %refs_2_.3), custom_call_target="tpu_custom_call" | custom-call | tf_op jit(solution)/shard_map/pack_twin/pallas_call | solution.py:25
  6.1 0.7 copy-done.17
  6.8 2.3 %pack.2 = (bf16[2,2,128,128]{3,2,1,0:T(8,128)(2,1)}, bf16[2,2,128,128]{3,2,1,0:T(8,128)(2,1)}, bf16[2,2,128,128]{3,2,1,0:T(8,128)(2,1)}, bf16[2,2,128,128]{3,2,1,0:T(8,128)(2,1)}) custom-call(s32[2]{0:T(128)} %pad_add_fusion.place_ref, bf16[128,3072]{1,0:T(8,128)(2,1)} %refs_0_.7, bf16[128,3072]{1,0:T(8,128)(2,1)} %refs_1_.7, bf16[4,2,128,128]{3,2,1,0:T(8,128)(2,1)} %copy-done.17), custom_call_target="tpu_custom_call" | custom-call | tf_op jit(solution)/shard_map/pack/pallas_call | solution.py:25
  9.2 0.1 add.86
  9.3 0.1 add_multiply_fusion.1
  9.3 3.0 %collective-permute-start.2 = (bf16[2,2,128,128]{3,2,1,0:T(8,128)(2,1)}, bf16[2,2,128,128]{3,2,1,0:T(8,128)(2,1)S(1)}, u32[]{:S(2)}, u32[]{:S(2)}) collective-permute-start(bf16[2,2,128,128]{3,2,1,0:T(8,128)(2,1)} %get-tuple-element.72), channel_id=1, source_target_pairs={{0,1},{1,0},{2,3},{3,2},{4,5},{5,4},{6,7},{7,6},{8,9},{9,8},{10,11... | collective-permute-start | bytes 393224 | tf_op jit(solution)/shard_map/ppermute | solution.py:275
  12.4 2.6 %collective-permute-start.4 = (bf16[2,2,128,128]{3,2,1,0:T(8,128)(2,1)}, bf16[2,2,128,128]{3,2,1,0:T(8,128)(2,1)S(1)}, u32[]{:S(2)}, u32[]{:S(2)}) collective-permute-start(bf16[2,2,128,128]{3,2,1,0:T(8,128)(2,1)} %get-tuple-element.75), channel_id=1, source_target_pairs={{0,2},{1,3},{2,0},{3,1},{4,6},{5,7},{6,4},{7,5},{8,10},{9,11},{10,... | collective-permute-start | bytes 393224 | tf_op jit(solution)/shard_map/ppermute | solution.py:275
  15.0 1.0 copy-done.15
  16.0 3.2 %pack.3 = (bf16[2,3,128,128]{3,2,1,0:T(8,128)(2,1)}, bf16[2,3,128,128]{3,2,1,0:T(8,128)(2,1)}, bf16[2,3,128,128]{3,2,1,0:T(8,128)(2,1)}, bf16[2,3,128,128]{3,2,1...) custom-call(s32[2]{0:T(128)} %pad_add_fusion.place_ref, ...), custom_call_target="tpu_custom_call" | custom-call | tf_op jit(solution)/shard_map/pack/pallas_call | solution.py:25
  19.3 6.2 %collective-permute-done.4 = bf16[2,2,128,128]{3,2,1,0:T(8,128)(2,1)S(1)} collective-permute-done((bf16[2,2,128,128]{3,2,1,0:T(8,128)(2,1)}, bf16[2,2,128,128]{3,2,1,0:T(8,128)(2,1)S(1)}, u32[]{:S(2)}, u32[]{:S(2)}) %collective-permute-start.4) | collective-permute-done | bytes 131104 | tf_op jit(solution)/shard_map/ppermute | solution.py:275
  25.5 0.1 pad_maximum_fusion
  25.6 1.6 %collective-permute-start.8 = (bf16[4,2,2,128,128]{4,3,2,1,0:T(8,128)(2,1)S(1)}, bf16[4,2,2,128,128]{4,3,2,1,0:T(8,128)(2,1)S(1)}, u32[]{:S(2)}, u32[]{:S(2)}) collective-permute-start(bf16[4,2,2,128,128]{4,3,2,1,0:T(8,128)(2,1)S(1)} %get-tuple-element.135), channel_id=1, source_target_pairs={{0,8},{4,20},{8,0},{12,28},{16,24},{20,4},{24,16},{28,12},{1,9},{5... | collective-permute-start | bytes 1572872 | tf_op jit(solution)/shard_map/ppermute | solution.py:278
  27.2 1.5 %collective-permute-start.9 = (bf16[4,2,2,128,128]{4,3,2,1,0:T(8,128)(2,1)S(1)}, bf16[4,2,2,128,128]{4,3,2,1,0:T(8,128)(2,1)S(1)}, u32[]{:S(2)}, u32[]{:S(2)}) collective-permute-start(bf16[4,2,2,128,128]{4,3,2,1,0:T(8,128)(2,1)S(1)} %get-tuple-element.135), channel_id=1, source_target_pairs={{0,16},{4,12},{8,24},{12,4},{16,0},{20,28},{24,8},{28,20},{1,17},{... | collective-permute-start | bytes 1572872 | tf_op jit(solution)/shard_map/ppermute | solution.py:278
  28.7 0.1 add.87
  28.8 0.1 add.88
  28.8 2.4 %collective-permute-start.7 = (bf16[2,3,128,128]{3,2,1,0:T(8,128)(2,1)S(1)}, bf16[2,3,128,128]{3,2,1,0:T(8,128)(2,1)S(1)}, u32[]{:S(2)}, u32[]{:S(2)}) collective-permute-start(bf16[2,3,128,128]{3,2,1,0:T(8,128)(2,1)S(1)} %copy-done.33), channel_id=1, source_target_pairs={{0,3},{1,2},{2,1},{3,0},{4,7},{5,6},{6,5},{7,4},{8,11},{9,10},{10,... | collective-permute-start | bytes 589832 | tf_op jit(solution)/shard_map/ppermute | solution.py:275
  31.3 0.1 add.97.key_ids_ref
  31.4 1.4 %collective-permute-start.3 = (bf16[2,3,128,128]{3,2,1,0:T(8,128)(2,1)S(1)}, bf16[2,3,128,128]{3,2,1,0:T(8,128)(2,1)S(1)}, u32[]{:S(2)}, u32[]{:S(2)}) collective-permute-start(bf16[2,3,128,128]{3,2,1,0:T(8,128)(2,1)S(1)} %copy-done.31), channel_id=1, source_target_pairs={{0,1},{1,0},{2,3},{3,2},{4,5},{5,4},{6,7},{7,6},{8,9},{9,8},{10,11... | collective-permute-start | bytes 589832 | tf_op jit(solution)/shard_map/ppermute | solution.py:275
  32.8 0.7 collective-permute-start.5
  33.5 5.1 %collective-permute-done.7.refs_3_ = bf16[2,3,128,128]{3,2,1,0:T(8,128)(2,1)S(1)} collective-permute-done((bf16[2,3,128,128]{3,2,1,0:T(8,128)(2,1)S(1)}, bf16[2,3,128,128]{3,2,1,0:T(8,128)(2,1)S(1)}, u32[]{:S(2)}, u32[]{:S(2)}) %collective-permute-start.7) | collective-permute-done | bytes 196640 | tf_op jit(solution)/shard_map/ppermute | solution.py:275
  38.7 0.7 collective-permute-start.10
  39.3 1.5 %collective-permute-start.11 = (bf16[2,2,2,128,128]{4,3,2,1,0:T(8,128)(2,1)S(1)}, bf16[2,2,2,128,128]{4,3,2,1,0:T(8,128)(2,1)S(1)}, u32[]{:S(2)}, u32[]{:S(2)}) collective-permute-start(bf16[2,2,2,128,128]{4,3,2,1,0:T(8,128)(2,1)S(1)} %slice.105), channel_id=1, source_target_pairs={{0,8},{4,20},{8,0},{12,28},{16,24},{20,4},{24,16},{28,12},{1,9},{5... | collective-permute-start | bytes 786440 | tf_op jit(solution)/shard_map/ppermute | solution.py:278
  40.8 6.5 %collective-permute-done.5.refs_2_ = bf16[2,3,128,128]{3,2,1,0:T(8,128)(2,1)S(1)} collective-permute-done((bf16[2,3,128,128]{3,2,1,0:T(8,128)(2,1)S(1)}, bf16[2,3,128,128]{3,2,1,0:T(8,128)(2,1)S(1)}, u32[]{:S(2)}, u32[]{:S(2)}) %collective-permute-start.5) | collective-permute-done | bytes 196640 | tf_op jit(solution)/shard_map/ppermute | solution.py:275
  47.4 0.9 copy-done.7
  48.4 0.1 fusion.1
  48.5 0.6 collective-permute-start.12
  49.1 0.6 collective-permute-start.13
  49.7 2.5 %collective-permute-start.18 = (bf16[2,3,128,128]{3,2,1,0:T(8,128)(2,1)S(1)}, bf16[2,3,128,128]{3,2,1,0:T(8,128)(2,1)S(1)}, u32[]{:S(2)}, u32[]{:S(2)}) collective-permute-start(bf16[2,3,128,128]{3,2,1,0:T(8,128)(2,1)S(1)} %copy-done.30), channel_id=1, source_target_pairs={{0,3},{1,2},{2,1},{3,0},{4,7},{5,6},{6,5},{7,4},{8,11},{9,10},{10,... | collective-permute-start | bytes 589832 | tf_op jit(solution)/shard_map/ppermute | solution.py:275
  52.1 5.3 %collective-permute-start.17 = (bf16[2,3,128,128]{3,2,1,0:T(8,128)(2,1)S(1)}, bf16[2,3,128,128]{3,2,1,0:T(8,128)(2,1)S(1)}, u32[]{:S(2)}, u32[]{:S(2)}) collective-permute-start(bf16[2,3,128,128]{3,2,1,0:T(8,128)(2,1)S(1)} %copy-done.29), channel_id=1, source_target_pairs={{0,2},{1,3},{2,0},{3,1},{4,6},{5,7},{6,4},{7,5},{8,10},{9,11},{10,... | collective-permute-start | bytes 589832 | tf_op jit(solution)/shard_map/ppermute | solution.py:275
  57.5 0.6 copy-done.8
  58.1 9.4 %attend.4 = (bf16[2,2,128,128]{3,2,1,0:T(8,128)(2,1)S(1)}, bf16[2,2,128,128]{3,2,1,0:T(8,128)(2,1)S(1)}, bf16[2,2,128,128]{3,2,1,0:T(8,128)(2,1)S(1)}, bf16[2,2,128,128]{3,2,1,0:T(8,128)(2,1)S(1)}) custom-call(s32[2]{0:T(128)S(1)} %copy-done.8, s32[32]{0:T(128)S(1)} %copy-done.14, s32[8]{0:T(128)S(1)} %add.89.query_ids_ref, s32[32]{0:T(128)S(1)} %add.97.key_ids_ref, ...), custom_call_target="tpu_custom_call" | custom-call | flops 21474836480 | bytes 2097152 | tf_op jit(solution)/shard_map/attend/pallas_call | solution.py:209
  67.6 0.7 collective-permute-start.14
  68.3 1.5 %collective-permute-start.15 = (bf16[2,2,2,128,128]{4,3,2,1,0:T(8,128)(2,1)S(1)}, bf16[2,2,2,128,128]{4,3,2,1,0:T(8,128)(2,1)S(1)}, u32[]{:S(2)}, u32[]{:S(2)}) collective-permute-start(bf16[2,2,2,128,128]{4,3,2,1,0:T(8,128)(2,1)S(1)} %slice.110), channel_id=1, source_target_pairs={{0,8},{4,20},{8,0},{12,28},{16,24},{20,4},{24,16},{28,12},{1,9},{5... | collective-permute-start | bytes 786440 | tf_op jit(solution)/shard_map/ppermute | solution.py:278
  69.9 6.9 %collective-permute-done.14 = bf16[2,2,2,128,128]{4,3,2,1,0:T(8,128)(2,1)S(1)} collective-permute-done((bf16[2,2,2,128,128]{4,3,2,1,0:T(8,128)(2,1)S(1)}, bf16[2,2,2,128,128]{4,3,2,1,0:T(8,128)(2,1)S(1)}, u32[]{:S(2)}, u32[]{:S(2)}) %collective-permute-start.14) | collective-permute-done | bytes 262176 | tf_op jit(solution)/shard_map/ppermute | solution.py:278
  76.8 0.7 collective-permute-done.15
  77.5 0.1 fusion
  77.6 1.5 %collective-permute-start.22 = (bf16[4,2,2,128,128]{4,3,2,1,0:T(8,128)(2,1)S(1)}, bf16[4,2,2,128,128]{4,3,2,1,0:T(8,128)(2,1)S(1)}, u32[]{:S(2)}, u32[]{:S(2)}) collective-permute-start(bf16[4,2,2,128,128]{4,3,2,1,0:T(8,128)(2,1)S(1)} %get-tuple-element.132), channel_id=1, source_target_pairs={{0,8},{4,20},{8,0},{12,28},{16,24},{20,4},{24,16},{28,12},{1,9},{5... | collective-permute-start | bytes 1572872 | tf_op jit(solution)/shard_map/ppermute | solution.py:278
  79.1 1.5 %collective-permute-start.23 = (bf16[4,2,2,128,128]{4,3,2,1,0:T(8,128)(2,1)S(1)}, bf16[4,2,2,128,128]{4,3,2,1,0:T(8,128)(2,1)S(1)}, u32[]{:S(2)}, u32[]{:S(2)}) collective-permute-start(bf16[4,2,2,128,128]{4,3,2,1,0:T(8,128)(2,1)S(1)} %get-tuple-element.132), channel_id=1, source_target_pairs={{0,16},{4,12},{8,24},{12,4},{16,0},{20,28},{24,8},{28,20},{1,17},{... | collective-permute-start | bytes 1572872 | tf_op jit(solution)/shard_map/ppermute | solution.py:278
  80.6 1.6 %collective-permute-start.19 = (bf16[2,2,128,128]{3,2,1,0:T(8,128)(2,1)S(1)}, bf16[2,2,128,128]{3,2,1,0:T(8,128)(2,1)S(1)}, u32[]{:S(2)}, u32[]{:S(2)}) collective-permute-start(bf16[2,2,128,128]{3,2,1,0:T(8,128)(2,1)S(1)} %get-tuple-element.107), channel_id=1, source_target_pairs={{0,1},{1,0},{2,3},{3,2},{4,5},{5,4},{6,7},{7,6},{8,9},{9,8},{10,11... | collective-permute-start | bytes 393224 | tf_op jit(solution)/shard_map/ppermute | solution.py:275
  82.2 1.2 collective-permute-start.20
  83.4 1.6 %collective-permute-start.21 = (bf16[2,2,128,128]{3,2,1,0:T(8,128)(2,1)S(1)}, bf16[2,2,128,128]{3,2,1,0:T(8,128)(2,1)S(1)}, u32[]{:S(2)}, u32[]{:S(2)}) collective-permute-start(bf16[2,2,128,128]{3,2,1,0:T(8,128)(2,1)S(1)} %get-tuple-element.109), channel_id=1, source_target_pairs={{0,3},{1,2},{2,1},{3,0},{4,7},{5,6},{6,5},{7,4},{8,11},{9,10},{10,... | collective-permute-start | bytes 393224 | tf_op jit(solution)/shard_map/ppermute | solution.py:275
  85.0 9.2 %attend.5 = (bf16[2,1,128,128]{3,2,1,0:T(8,128)(2,1)S(1)}, bf16[2,1,128,128]{3,2,1,0:T(8,128)(2,1)S(1)}, bf16[2,1,128,128]{3,2,1,0:T(8,128)(2,1)S(1)}, bf16[2,1,128,128]{3,2,1,0:T(8,128)(2,1)S(1)}) custom-call(s32[2]{0:T(128)S(1)} %copy-done.8, s32[32]{0:T(128)S(1)} %copy-done.14, s32[8]{0:T(128)S(1)} %add.89.query_ids_ref, s32[32]{0:T(128)S(1)} %add.97.key_ids_ref, ...), custom_call_target="tpu_custom_call" | custom-call | flops 21474836480 | bytes 2097152 | tf_op jit(solution)/shard_map/attend/pallas_call | solution.py:209
  94.4 0.7 collective-permute-start.27
  95.2 0.5 collective-permute-start.28
  95.7 1.8 %collective-permute-start.24 = (bf16[2,1,128,128]{3,2,1,0:T(8,128)(2,1)S(1)}, bf16[2,1,128,128]{3,2,1,0:T(8,128)(2,1)S(1)}, u32[]{:S(2)}, u32[]{:S(2)}) collective-permute-start(bf16[2,1,128,128]{3,2,1,0:T(8,128)(2,1)S(1)} %get-tuple-element.118), channel_id=1, source_target_pairs={{0,1},{1,0},{2,3},{3,2},{4,5},{5,4},{6,7},{7,6},{8,9},{9,8},{10,11... | collective-permute-start | bytes 196616 | tf_op jit(solution)/shard_map/ppermute | solution.py:275
  97.5 1.0 collective-permute-start.25
  98.6 1.5 %collective-permute-start.26 = (bf16[2,1,128,128]{3,2,1,0:T(8,128)(2,1)S(1)}, bf16[2,1,128,128]{3,2,1,0:T(8,128)(2,1)S(1)}, u32[]{:S(2)}, u32[]{:S(2)}) collective-permute-start(bf16[2,1,128,128]{3,2,1,0:T(8,128)(2,1)S(1)} %get-tuple-element.120), channel_id=1, source_target_pairs={{0,3},{1,2},{2,1},{3,0},{4,7},{5,6},{6,5},{7,4},{8,11},{9,10},{10,... | collective-permute-start | bytes 196616 | tf_op jit(solution)/shard_map/ppermute | solution.py:275
  100.1 6.6 %attend.6 = (f32[1024,128]{1,0:T(8,128)S(1)}, f32[1024,128]{1,0:T(8,128)S(1)}, f32[1024,128]{1,0:T(8,128)S(1)}) custom-call(s32[2]{0:T(128)S(1)} %copy-done.8, s32[32]{0:T(128)S(1)} %copy-done.14, s32[8]{0:T(128)S(1)} %add.89.query_ids_ref, s32[32]{0:T(128)S(1)} %add.97.key_ids_ref, s32[6,32,32]{2,1,0:T(8,128)S(1)} %copy-done.9, ...), custom_call_target="tpu_custom_call" | custom-call | flops 16106127360 | bytes 1572864 | tf_op jit(solution)/shard_map/attend/pallas_call | solution.py:209
  106.7 0.6 copy-done.20
  107.4 0.6 copy-done.18
  108.0 3.5 %attend.7 = (bf16[2,1,128,128]{3,2,1,0:T(8,128)(2,1)S(1)}, bf16[2,1,128,128]{3,2,1,0:T(8,128)(2,1)S(1)}, bf16[2,1,128,128]{3,2,1,0:T(8,128)(2,1)S(1)}, bf16[2,1,128,128]{3,2,1,0:T(8,128)(2,1)S(1)}) custom-call(s32[2]{0:T(128)S(1)} %copy-done.8, s32[32]{0:T(128)S(1)} %copy-done.14, s32[8]{0:T(128)S(1)} %add.89.query_ids_ref, s32[32]{0:T(128)S(1)} %add.97.key_ids_ref, ...), custom_call_target="tpu_custom_call" | custom-call | flops 5368709120 | bytes 524288 | tf_op jit(solution)/shard_map/attend/pallas_call | solution.py:209
  111.5 1.0 collective-permute-start.29
  112.5 2.0 %collective-permute-start.30 = (bf16[2,1,128,128]{3,2,1,0:T(8,128)(2,1)S(1)}, bf16[2,1,128,128]{3,2,1,0:T(8,128)(2,1)S(1)}, u32[]{:S(2)}, u32[]{:S(2)}) collective-permute-start(bf16[2,1,128,128]{3,2,1,0:T(8,128)(2,1)S(1)} %get-tuple-element.126), channel_id=1, source_target_pairs={{0,2},{1,3},{2,0},{3,1},{4,6},{5,7},{6,4},{7,5},{8,10},{9,11},{10,... | collective-permute-start | bytes 196616 | tf_op jit(solution)/shard_map/ppermute | solution.py:275
  114.4 1.5 %collective-permute-start.31 = (bf16[2,1,128,128]{3,2,1,0:T(8,128)(2,1)S(1)}, bf16[2,1,128,128]{3,2,1,0:T(8,128)(2,1)S(1)}, u32[]{:S(2)}, u32[]{:S(2)}) collective-permute-start(bf16[2,1,128,128]{3,2,1,0:T(8,128)(2,1)S(1)} %get-tuple-element.127), channel_id=1, source_target_pairs={{0,3},{1,2},{2,1},{3,0},{4,7},{5,6},{6,5},{7,4},{8,11},{9,10},{10,... | collective-permute-start | bytes 196616 | tf_op jit(solution)/shard_map/ppermute | solution.py:275
  116.0 0.5 collective-permute-start.33
  116.5 4.0 %collective-permute-done.31.refs_11_ = bf16[2,1,128,128]{3,2,1,0:T(8,128)(2,1)S(1)} collective-permute-done((bf16[2,1,128,128]{3,2,1,0:T(8,128)(2,1)S(1)}, bf16[2,1,128,128]{3,2,1,0:T(8,128)(2,1)S(1)}, u32[]{:S(2)}, u32[]{:S(2)}) %collective-permute-start.31) | collective-permute-done | bytes 65568 | tf_op jit(solution)/shard_map/ppermute | solution.py:275
  120.6 0.6 copy-done.23
  121.2 0.6 copy-done.21
  121.8 1.3 %collective-permute-done.34.refs_14_ = bf16[4,128,128]{2,1,0:T(8,128)(2,1)S(1)} collective-permute-done((bf16[4,128,128]{2,1,0:T(8,128)(2,1)S(1)}, bf16[4,128,128]{2,1,0:T(8,128)(2,1)S(1)}, u32[]{:S(2)}, u32[]{:S(2)}) %collective-permute-start.34) | collective-permute-done | bytes 131104 | tf_op jit(solution)/shard_map/ppermute | solution.py:278
  123.1 0.7 copy-done.27
  123.8 2.5 %unpack.1 = bf16[128,3072]{1,0:T(8,128)(2,1)} custom-call(s32[2]{0:T(128)} %pad_add_fusion.place_ref, bf16[2,2,128,128]{3,2,1,0:T(8,128)(2,1)} %copy-done, bf16[2,2,128,128]{3,2,1,0:T(8,128)(2,1)} %copy-done.1, bf16[2,2,128,128]{3,2,1,0:T(8,128)(2,1)} %copy-done.2, bf16[2,2,128,128]{3,2,1,0:T(8,128)(2,1)} %copy-done.3, bf16[2,1,128,128]{3,2,1,0:T(8,128)(2,1)} %copy-done.4, ...), custom_call_target="tpu_custom_call" | custom-call | tf_op jit(solution)/shard_map/unpack/pallas_call | solution.py:25
  (127 shorter events, 0.7 us)
Async XLA Ops:
  2.8 3.3 %collective-permute-start = (bf16[4,2,128,128]{3,2,1,0:T(8,128)(2,1)}, bf16[4,2,128,128]{3,2,1,0:T(8,128)(2,1)S(1)}, u32[]{:S(2)}, u32[]{:S(2)}) collective-permute-start(bf16[4,2,128,128]{3,2,1,0:T(8,128)(2,1)} %pack_twin.3), channel_id=1, source_target_pairs={{0,4},{4,0},{8,12},{12,8},{16,20},{20,16},{24,28},{28,24},{1,5},{5... | collective-permute-start | bytes 786440 | tf_op jit(solution)/shard_map/ppermute | solution.py:278
  6.1 3.0 %copy-start.16 = (bf16[4,7,128,128]{3,2,1,0:T(8,128)(2,1)S(1)}, bf16[4,7,128,128]{3,2,1,0:T(8,128)(2,1)}, u32[]{:S(2)}) copy-start(bf16[4,7,128,128]{3,2,1,0:T(8,128)(2,1)} %pack_twin.2) | copy-start | bytes 2752516
  6.1 0.7 copy-start.17
  9.1 5.9 %collective-permute-start.1 = (bf16[4,7,128,128]{3,2,1,0:T(8,128)(2,1)S(1)}, bf16[4,7,128,128]{3,2,1,0:T(8,128)(2,1)S(1)}, u32[]{:S(2)}, u32[]{:S(2)}) collective-permute-start(bf16[4,7,128,128]{3,2,1,0:T(8,128)(2,1)S(1)} %copy-done.16), channel_id=1, source_target_pairs={{0,4},{4,0},{8,12},{12,8},{16,20},{20,16},{24,28},{28,24},{1,5},{5... | collective-permute-start | bytes 2752520 | tf_op jit(solution)/shard_map/ppermute | solution.py:278
  9.3 9.9 %collective-permute-start.2 = (bf16[2,2,128,128]{3,2,1,0:T(8,128)(2,1)}, bf16[2,2,128,128]{3,2,1,0:T(8,128)(2,1)S(1)}, u32[]{:S(2)}, u32[]{:S(2)}) collective-permute-start(bf16[2,2,128,128]{3,2,1,0:T(8,128)(2,1)} %get-tuple-element.72), channel_id=1, source_target_pairs={{0,1},{1,0},{2,3},{3,2},{4,5},{5,4},{6,7},{7,6},{8,9},{9,8},{10,11... | collective-permute-start | bytes 393224 | tf_op jit(solution)/shard_map/ppermute | solution.py:275
  12.4 13.1 %collective-permute-start.4 = (bf16[2,2,128,128]{3,2,1,0:T(8,128)(2,1)}, bf16[2,2,128,128]{3,2,1,0:T(8,128)(2,1)S(1)}, u32[]{:S(2)}, u32[]{:S(2)}) collective-permute-start(bf16[2,2,128,128]{3,2,1,0:T(8,128)(2,1)} %get-tuple-element.75), channel_id=1, source_target_pairs={{0,2},{1,3},{2,0},{3,1},{4,6},{5,7},{6,4},{7,5},{8,10},{9,11},{10,... | collective-permute-start | bytes 393224 | tf_op jit(solution)/shard_map/ppermute | solution.py:275
  14.9 10.5 %collective-permute-start.6 = (bf16[2,2,128,128]{3,2,1,0:T(8,128)(2,1)}, bf16[2,2,128,128]{3,2,1,0:T(8,128)(2,1)S(1)}, u32[]{:S(2)}, u32[]{:S(2)}) collective-permute-start(bf16[2,2,128,128]{3,2,1,0:T(8,128)(2,1)} %get-tuple-element.78), channel_id=1, source_target_pairs={{0,3},{1,2},{2,1},{3,0},{4,7},{5,6},{6,5},{7,4},{8,11},{9,10},{10,... | collective-permute-start | bytes 393224 | tf_op jit(solution)/shard_map/ppermute | solution.py:275
  15.0 10.5 %copy-start.24 = (bf16[2,2,128,128]{3,2,1,0:T(8,128)(2,1)S(1)}, bf16[2,2,128,128]{3,2,1,0:T(8,128)(2,1)}, u32[]{:S(2)}) copy-start(bf16[2,2,128,128]{3,2,1,0:T(8,128)(2,1)} %get-tuple-element.80) | copy-start | bytes 393220
  15.0 1.0 copy-start.15
  25.5 3.4 %copy-start.33 = (bf16[2,3,128,128]{3,2,1,0:T(8,128)(2,1)S(1)}, bf16[2,3,128,128]{3,2,1,0:T(8,128)(2,1)}, u32[]{:S(2)}) copy-start(bf16[2,3,128,128]{3,2,1,0:T(8,128)(2,1)} %get-tuple-element.79) | copy-start | bytes 589828
  25.5 5.9 %copy-start.31 = (bf16[2,3,128,128]{3,2,1,0:T(8,128)(2,1)S(1)}, bf16[2,3,128,128]{3,2,1,0:T(8,128)(2,1)}, u32[]{:S(2)}) copy-start(bf16[2,3,128,128]{3,2,1,0:T(8,128)(2,1)} %get-tuple-element.73) | copy-start | bytes 589828
  25.5 7.3 %copy-start.32 = (bf16[2,3,128,128]{3,2,1,0:T(8,128)(2,1)S(1)}, bf16[2,3,128,128]{3,2,1,0:T(8,128)(2,1)}, u32[]{:S(2)}) copy-start(bf16[2,3,128,128]{3,2,1,0:T(8,128)(2,1)} %get-tuple-element.76) | copy-start | bytes 589828
  25.6 13.0 %collective-permute-start.8 = (bf16[4,2,2,128,128]{4,3,2,1,0:T(8,128)(2,1)S(1)}, bf16[4,2,2,128,128]{4,3,2,1,0:T(8,128)(2,1)S(1)}, u32[]{:S(2)}, u32[]{:S(2)}) collective-permute-start(bf16[4,2,2,128,128]{4,3,2,1,0:T(8,128)(2,1)S(1)} %get-tuple-element.135), channel_id=1, source_target_pairs={{0,8},{4,20},{8,0},{12,28},{16,24},{20,4},{24,16},{28,12},{1,9},{5... | collective-permute-start | bytes 1572872 | tf_op jit(solution)/shard_map/ppermute | solution.py:278
  27.2 11.5 %collective-permute-start.9 = (bf16[4,2,2,128,128]{4,3,2,1,0:T(8,128)(2,1)S(1)}, bf16[4,2,2,128,128]{4,3,2,1,0:T(8,128)(2,1)S(1)}, u32[]{:S(2)}, u32[]{:S(2)}) collective-permute-start(bf16[4,2,2,128,128]{4,3,2,1,0:T(8,128)(2,1)S(1)} %get-tuple-element.135), channel_id=1, source_target_pairs={{0,16},{4,12},{8,24},{12,4},{16,0},{20,28},{24,8},{28,20},{1,17},{... | collective-permute-start | bytes 1572872 | tf_op jit(solution)/shard_map/ppermute | solution.py:278
  28.8 9.7 %collective-permute-start.7 = (bf16[2,3,128,128]{3,2,1,0:T(8,128)(2,1)S(1)}, bf16[2,3,128,128]{3,2,1,0:T(8,128)(2,1)S(1)}, u32[]{:S(2)}, u32[]{:S(2)}) collective-permute-start(bf16[2,3,128,128]{3,2,1,0:T(8,128)(2,1)S(1)} %copy-done.33), channel_id=1, source_target_pairs={{0,3},{1,2},{2,1},{3,0},{4,7},{5,6},{6,5},{7,4},{8,11},{9,10},{10,... | collective-permute-start | bytes 589832 | tf_op jit(solution)/shard_map/ppermute | solution.py:275
  31.4 15.9 %collective-permute-start.3 = (bf16[2,3,128,128]{3,2,1,0:T(8,128)(2,1)S(1)}, bf16[2,3,128,128]{3,2,1,0:T(8,128)(2,1)S(1)}, u32[]{:S(2)}, u32[]{:S(2)}) collective-permute-start(bf16[2,3,128,128]{3,2,1,0:T(8,128)(2,1)S(1)} %copy-done.31), channel_id=1, source_target_pairs={{0,1},{1,0},{2,3},{3,2},{4,5},{5,4},{6,7},{7,6},{8,9},{9,8},{10,11... | collective-permute-start | bytes 589832 | tf_op jit(solution)/shard_map/ppermute | solution.py:275
  32.8 14.5 %collective-permute-start.5 = (bf16[2,3,128,128]{3,2,1,0:T(8,128)(2,1)S(1)}, bf16[2,3,128,128]{3,2,1,0:T(8,128)(2,1)S(1)}, u32[]{:S(2)}, u32[]{:S(2)}) collective-permute-start(bf16[2,3,128,128]{3,2,1,0:T(8,128)(2,1)S(1)} %copy-done.32), channel_id=1, source_target_pairs={{0,2},{1,3},{2,0},{3,1},{4,6},{5,7},{6,4},{7,5},{8,10},{9,11},{10,... | collective-permute-start | bytes 589832 | tf_op jit(solution)/shard_map/ppermute | solution.py:275
  38.7 8.7 %collective-permute-start.10 = (bf16[2,2,2,128,128]{4,3,2,1,0:T(8,128)(2,1)S(1)}, bf16[2,2,2,128,128]{4,3,2,1,0:T(8,128)(2,1)S(1)}, u32[]{:S(2)}, u32[]{:S(2)}) collective-permute-start(bf16[2,2,2,128,128]{4,3,2,1,0:T(8,128)(2,1)S(1)} %slice.104), channel_id=1, source_target_pairs={{0,16},{4,12},{8,24},{12,4},{16,0},{20,28},{24,8},{28,20},{1,17},{... | collective-permute-start | bytes 786440 | tf_op jit(solution)/shard_map/ppermute | solution.py:278
  39.3 8.1 %collective-permute-start.11 = (bf16[2,2,2,128,128]{4,3,2,1,0:T(8,128)(2,1)S(1)}, bf16[2,2,2,128,128]{4,3,2,1,0:T(8,128)(2,1)S(1)}, u32[]{:S(2)}, u32[]{:S(2)}) collective-permute-start(bf16[2,2,2,128,128]{4,3,2,1,0:T(8,128)(2,1)S(1)} %slice.105), channel_id=1, source_target_pairs={{0,8},{4,20},{8,0},{12,28},{16,24},{20,4},{24,16},{28,12},{1,9},{5... | collective-permute-start | bytes 786440 | tf_op jit(solution)/shard_map/ppermute | solution.py:278
  47.3 0.9 copy-start.7
  48.3 1.4 %copy-start.30 = (bf16[2,3,128,128]{3,2,1,0:T(8,128)(2,1)S(1)}, bf16[2,3,128,128]{3,2,1,0:T(8,128)(2,1)}, u32[]{:S(2)}) copy-start(bf16[2,3,128,128]{3,2,1,0:T(8,128)(2,1)} %get-tuple-element.105) | copy-start | bytes 589828
  48.3 3.8 %copy-start.29 = (bf16[2,3,128,128]{3,2,1,0:T(8,128)(2,1)S(1)}, bf16[2,3,128,128]{3,2,1,0:T(8,128)(2,1)}, u32[]{:S(2)}) copy-start(bf16[2,3,128,128]{3,2,1,0:T(8,128)(2,1)} %get-tuple-element.102) | copy-start | bytes 589828
  48.3 9.1 %copy-start.28 = (bf16[2,3,128,128]{3,2,1,0:T(8,128)(2,1)S(1)}, bf16[2,3,128,128]{3,2,1,0:T(8,128)(2,1)}, u32[]{:S(2)}) copy-start(bf16[2,3,128,128]{3,2,1,0:T(8,128)(2,1)} %get-tuple-element.99) | copy-start | bytes 589828
  48.3 9.1 %copy-start.9 = (s32[6,32,32]{2,1,0:T(8,128)S(1)}, s32[6,32,32]{2,1,0:T(8,128)}, u32[]{:S(2)}) copy-start(s32[6,32,32]{2,1,0:T(8,128)} %mask_ref.7) | copy-start | bytes 73732
  48.3 9.1 %copy-start.10 = (bf16[2,1,128,128]{3,2,1,0:T(8,128)(2,1)S(1)}, bf16[2,1,128,128]{3,2,1,0:T(8,128)(2,1)}, u32[]{:S(2)}) copy-start(bf16[2,1,128,128]{3,2,1,0:T(8,128)(2,1)} %get-tuple-element.85.refs_9_) | copy-start | bytes 196612
  48.3 9.1 %copy-start.11 = (bf16[2,1,128,128]{3,2,1,0:T(8,128)(2,1)S(1)}, bf16[2,1,128,128]{3,2,1,0:T(8,128)(2,1)}, u32[]{:S(2)}) copy-start(bf16[2,1,128,128]{3,2,1,0:T(8,128)(2,1)} %get-tuple-element.86.refs_10_) | copy-start | bytes 196612
  48.4 9.1 %copy-start.12 = (bf16[2,1,128,128]{3,2,1,0:T(8,128)(2,1)S(1)}, bf16[2,1,128,128]{3,2,1,0:T(8,128)(2,1)}, u32[]{:S(2)}) copy-start(bf16[2,1,128,128]{3,2,1,0:T(8,128)(2,1)} %get-tuple-element.87.refs_11_) | copy-start | bytes 196612
  48.4 9.1 %copy-start.13 = (bf16[2,1,128,128]{3,2,1,0:T(8,128)(2,1)S(1)}, bf16[2,1,128,128]{3,2,1,0:T(8,128)(2,1)}, u32[]{:S(2)}) copy-start(bf16[2,1,128,128]{3,2,1,0:T(8,128)(2,1)} %get-tuple-element.88.refs_12_) | copy-start | bytes 196612
  48.5 19.1 %collective-permute-start.12 = (bf16[4,2,2,128,128]{4,3,2,1,0:T(8,128)(2,1)S(1)}, bf16[4,2,2,128,128]{4,3,2,1,0:T(8,128)(2,1)S(1)}, u32[]{:S(2)}, u32[]{:S(2)}) collective-permute-start(bf16[4,2,2,128,128]{4,3,2,1,0:T(8,128)(2,1)S(1)} %get-tuple-element.134), channel_id=1, source_target_pairs={{0,8},{4,20},{8,0},{12,28},{16,24},{20,4},{24,16},{28,12},{1,9},{5... | collective-permute-start | bytes 1572872 | tf_op jit(solution)/shard_map/ppermute | solution.py:278
  49.1 18.5 %collective-permute-start.13 = (bf16[4,2,2,128,128]{4,3,2,1,0:T(8,128)(2,1)S(1)}, bf16[4,2,2,128,128]{4,3,2,1,0:T(8,128)(2,1)S(1)}, u32[]{:S(2)}, u32[]{:S(2)}) collective-permute-start(bf16[4,2,2,128,128]{4,3,2,1,0:T(8,128)(2,1)S(1)} %get-tuple-element.134), channel_id=1, source_target_pairs={{0,16},{4,12},{8,24},{12,4},{16,0},{20,28},{24,8},{28,20},{1,17},{... | collective-permute-start | bytes 1572872 | tf_op jit(solution)/shard_map/ppermute | solution.py:278
  49.7 17.8 %collective-permute-start.18 = (bf16[2,3,128,128]{3,2,1,0:T(8,128)(2,1)S(1)}, bf16[2,3,128,128]{3,2,1,0:T(8,128)(2,1)S(1)}, u32[]{:S(2)}, u32[]{:S(2)}) collective-permute-start(bf16[2,3,128,128]{3,2,1,0:T(8,128)(2,1)S(1)} %copy-done.30), channel_id=1, source_target_pairs={{0,3},{1,2},{2,1},{3,0},{4,7},{5,6},{6,5},{7,4},{8,11},{9,10},{10,... | collective-permute-start | bytes 589832 | tf_op jit(solution)/shard_map/ppermute | solution.py:275
  52.1 17.7 %collective-permute-start.17 = (bf16[2,3,128,128]{3,2,1,0:T(8,128)(2,1)S(1)}, bf16[2,3,128,128]{3,2,1,0:T(8,128)(2,1)S(1)}, u32[]{:S(2)}, u32[]{:S(2)}) collective-permute-start(bf16[2,3,128,128]{3,2,1,0:T(8,128)(2,1)S(1)} %copy-done.29), channel_id=1, source_target_pairs={{0,2},{1,3},{2,0},{3,1},{4,6},{5,7},{6,4},{7,5},{8,10},{9,11},{10,... | collective-permute-start | bytes 589832 | tf_op jit(solution)/shard_map/ppermute | solution.py:275
  57.4 12.4 %collective-permute-start.16 = (bf16[2,3,128,128]{3,2,1,0:T(8,128)(2,1)S(1)}, bf16[2,3,128,128]{3,2,1,0:T(8,128)(2,1)S(1)}, u32[]{:S(2)}, u32[]{:S(2)}) collective-permute-start(bf16[2,3,128,128]{3,2,1,0:T(8,128)(2,1)S(1)} %copy-done.28), channel_id=1, source_target_pairs={{0,1},{1,0},{2,3},{3,2},{4,5},{5,4},{6,7},{7,6},{8,9},{9,8},{10,11... | collective-permute-start | bytes 589832 | tf_op jit(solution)/shard_map/ppermute | solution.py:275
  57.4 0.7 copy-start.8
  57.4 0.7 copy-start.14
  67.5 40.5 %copy-start = (bf16[2,2,128,128]{3,2,1,0:T(8,128)(2,1)}, bf16[2,2,128,128]{3,2,1,0:T(8,128)(2,1)S(1)}, u32[]{:S(2)}) copy-start(bf16[2,2,128,128]{3,2,1,0:T(8,128)(2,1)S(1)} %get-tuple-element.106.refs_0_) | copy-start | bytes 393220
  67.6 9.2 %collective-permute-start.14 = (bf16[2,2,2,128,128]{4,3,2,1,0:T(8,128)(2,1)S(1)}, bf16[2,2,2,128,128]{4,3,2,1,0:T(8,128)(2,1)S(1)}, u32[]{:S(2)}, u32[]{:S(2)}) collective-permute-start(bf16[2,2,2,128,128]{4,3,2,1,0:T(8,128)(2,1)S(1)} %slice.109), channel_id=1, source_target_pairs={{0,16},{4,12},{8,24},{12,4},{16,0},{20,28},{24,8},{28,20},{1,17},{... | collective-permute-start | bytes 786440 | tf_op jit(solution)/shard_map/ppermute | solution.py:278
  68.3 9.2 %collective-permute-start.15 = (bf16[2,2,2,128,128]{4,3,2,1,0:T(8,128)(2,1)S(1)}, bf16[2,2,2,128,128]{4,3,2,1,0:T(8,128)(2,1)S(1)}, u32[]{:S(2)}, u32[]{:S(2)}) collective-permute-start(bf16[2,2,2,128,128]{4,3,2,1,0:T(8,128)(2,1)S(1)} %slice.110), channel_id=1, source_target_pairs={{0,8},{4,20},{8,0},{12,28},{16,24},{20,4},{24,16},{28,12},{1,9},{5... | collective-permute-start | bytes 786440 | tf_op jit(solution)/shard_map/ppermute | solution.py:278
  69.8 7.7 %copy-start.6 = (bf16[2,3,128,128]{3,2,1,0:T(8,128)(2,1)S(1)}, bf16[2,3,128,128]{3,2,1,0:T(8,128)(2,1)}, u32[]{:S(2)}) copy-start(bf16[2,3,128,128]{3,2,1,0:T(8,128)(2,1)} %get-tuple-element.96.refs_0_) | copy-start | bytes 589828
  77.6 16.8 %collective-permute-start.22 = (bf16[4,2,2,128,128]{4,3,2,1,0:T(8,128)(2,1)S(1)}, bf16[4,2,2,128,128]{4,3,2,1,0:T(8,128)(2,1)S(1)}, u32[]{:S(2)}, u32[]{:S(2)}) collective-permute-start(bf16[4,2,2,128,128]{4,3,2,1,0:T(8,128)(2,1)S(1)} %get-tuple-element.132), channel_id=1, source_target_pairs={{0,8},{4,20},{8,0},{12,28},{16,24},{20,4},{24,16},{28,12},{1,9},{5... | collective-permute-start | bytes 1572872 | tf_op jit(solution)/shard_map/ppermute | solution.py:278
  79.1 15.3 %collective-permute-start.23 = (bf16[4,2,2,128,128]{4,3,2,1,0:T(8,128)(2,1)S(1)}, bf16[4,2,2,128,128]{4,3,2,1,0:T(8,128)(2,1)S(1)}, u32[]{:S(2)}, u32[]{:S(2)}) collective-permute-start(bf16[4,2,2,128,128]{4,3,2,1,0:T(8,128)(2,1)S(1)} %get-tuple-element.132), channel_id=1, source_target_pairs={{0,16},{4,12},{8,24},{12,4},{16,0},{20,28},{24,8},{28,20},{1,17},{... | collective-permute-start | bytes 1572872 | tf_op jit(solution)/shard_map/ppermute | solution.py:278
  80.6 13.7 %collective-permute-start.19 = (bf16[2,2,128,128]{3,2,1,0:T(8,128)(2,1)S(1)}, bf16[2,2,128,128]{3,2,1,0:T(8,128)(2,1)S(1)}, u32[]{:S(2)}, u32[]{:S(2)}) collective-permute-start(bf16[2,2,128,128]{3,2,1,0:T(8,128)(2,1)S(1)} %get-tuple-element.107), channel_id=1, source_target_pairs={{0,1},{1,0},{2,3},{3,2},{4,5},{5,4},{6,7},{7,6},{8,9},{9,8},{10,11... | collective-permute-start | bytes 393224 | tf_op jit(solution)/shard_map/ppermute | solution.py:275
  82.2 12.1 %collective-permute-start.20 = (bf16[2,2,128,128]{3,2,1,0:T(8,128)(2,1)S(1)}, bf16[2,2,128,128]{3,2,1,0:T(8,128)(2,1)S(1)}, u32[]{:S(2)}, u32[]{:S(2)}) collective-permute-start(bf16[2,2,128,128]{3,2,1,0:T(8,128)(2,1)S(1)} %get-tuple-element.108), channel_id=1, source_target_pairs={{0,2},{1,3},{2,0},{3,1},{4,6},{5,7},{6,4},{7,5},{8,10},{9,11},{10,... | collective-permute-start | bytes 393224 | tf_op jit(solution)/shard_map/ppermute | solution.py:275
  83.4 10.8 %collective-permute-start.21 = (bf16[2,2,128,128]{3,2,1,0:T(8,128)(2,1)S(1)}, bf16[2,2,128,128]{3,2,1,0:T(8,128)(2,1)S(1)}, u32[]{:S(2)}, u32[]{:S(2)}) collective-permute-start(bf16[2,2,128,128]{3,2,1,0:T(8,128)(2,1)S(1)} %get-tuple-element.109), channel_id=1, source_target_pairs={{0,3},{1,2},{2,1},{3,0},{4,7},{5,6},{6,5},{7,4},{8,11},{9,10},{10,... | collective-permute-start | bytes 393224 | tf_op jit(solution)/shard_map/ppermute | solution.py:275
  94.2 12.4 %copy-start.4 = (bf16[2,1,128,128]{3,2,1,0:T(8,128)(2,1)}, bf16[2,1,128,128]{3,2,1,0:T(8,128)(2,1)S(1)}, u32[]{:S(2)}) copy-start(bf16[2,1,128,128]{3,2,1,0:T(8,128)(2,1)S(1)} %get-tuple-element.117.refs_4_) | copy-start | bytes 196612
  94.2 13.7 %copy-start.3 = (bf16[2,2,128,128]{3,2,1,0:T(8,128)(2,1)}, bf16[2,2,128,128]{3,2,1,0:T(8,128)(2,1)S(1)}, u32[]{:S(2)}) copy-start(bf16[2,2,128,128]{3,2,1,0:T(8,128)(2,1)S(1)} %collective-permute-done.21.refs_3_) | copy-start | bytes 393220
  94.3 13.7 %copy-start.2 = (bf16[2,2,128,128]{3,2,1,0:T(8,128)(2,1)}, bf16[2,2,128,128]{3,2,1,0:T(8,128)(2,1)S(1)}, u32[]{:S(2)}) copy-start(bf16[2,2,128,128]{3,2,1,0:T(8,128)(2,1)S(1)} %collective-permute-done.20.refs_2_) | copy-start | bytes 393220
  94.3 13.7 %copy-start.1 = (bf16[2,2,128,128]{3,2,1,0:T(8,128)(2,1)}, bf16[2,2,128,128]{3,2,1,0:T(8,128)(2,1)S(1)}, u32[]{:S(2)}) copy-start(bf16[2,2,128,128]{3,2,1,0:T(8,128)(2,1)S(1)} %collective-permute-done.19.refs_1_) | copy-start | bytes 393220
  94.4 13.5 %collective-permute-start.27 = (bf16[2,2,2,128,128]{4,3,2,1,0:T(8,128)(2,1)S(1)}, bf16[2,2,2,128,128]{4,3,2,1,0:T(8,128)(2,1)S(1)}, u32[]{:S(2)}, u32[]{:S(2)}) collective-permute-start(bf16[2,2,2,128,128]{4,3,2,1,0:T(8,128)(2,1)S(1)} %slice.114), channel_id=1, source_target_pairs={{0,16},{4,12},{8,24},{12,4},{16,0},{20,28},{24,8},{28,20},{1,17},{... | collective-permute-start | bytes 786440 | tf_op jit(solution)/shard_map/ppermute | solution.py:278
  95.2 12.8 %collective-permute-start.28 = (bf16[2,2,2,128,128]{4,3,2,1,0:T(8,128)(2,1)S(1)}, bf16[2,2,2,128,128]{4,3,2,1,0:T(8,128)(2,1)S(1)}, u32[]{:S(2)}, u32[]{:S(2)}) collective-permute-start(bf16[2,2,2,128,128]{4,3,2,1,0:T(8,128)(2,1)S(1)} %slice.115), channel_id=1, source_target_pairs={{0,8},{4,20},{8,0},{12,28},{16,24},{20,4},{24,16},{28,12},{1,9},{5... | collective-permute-start | bytes 786440 | tf_op jit(solution)/shard_map/ppermute | solution.py:278
  95.7 11.6 %collective-permute-start.24 = (bf16[2,1,128,128]{3,2,1,0:T(8,128)(2,1)S(1)}, bf16[2,1,128,128]{3,2,1,0:T(8,128)(2,1)S(1)}, u32[]{:S(2)}, u32[]{:S(2)}) collective-permute-start(bf16[2,1,128,128]{3,2,1,0:T(8,128)(2,1)S(1)} %get-tuple-element.118), channel_id=1, source_target_pairs={{0,1},{1,0},{2,3},{3,2},{4,5},{5,4},{6,7},{7,6},{8,9},{9,8},{10,11... | collective-permute-start | bytes 196616 | tf_op jit(solution)/shard_map/ppermute | solution.py:275
  97.5 9.2 %collective-permute-start.25 = (bf16[2,1,128,128]{3,2,1,0:T(8,128)(2,1)S(1)}, bf16[2,1,128,128]{3,2,1,0:T(8,128)(2,1)S(1)}, u32[]{:S(2)}, u32[]{:S(2)}) collective-permute-start(bf16[2,1,128,128]{3,2,1,0:T(8,128)(2,1)S(1)} %get-tuple-element.119), channel_id=1, source_target_pairs={{0,2},{1,3},{2,0},{3,1},{4,6},{5,7},{6,4},{7,5},{8,10},{9,11},{10,... | collective-permute-start | bytes 196616 | tf_op jit(solution)/shard_map/ppermute | solution.py:275
  98.6 8.1 %collective-permute-start.26 = (bf16[2,1,128,128]{3,2,1,0:T(8,128)(2,1)S(1)}, bf16[2,1,128,128]{3,2,1,0:T(8,128)(2,1)S(1)}, u32[]{:S(2)}, u32[]{:S(2)}) collective-permute-start(bf16[2,1,128,128]{3,2,1,0:T(8,128)(2,1)S(1)} %get-tuple-element.120), channel_id=1, source_target_pairs={{0,3},{1,2},{2,1},{3,0},{4,7},{5,6},{6,5},{7,4},{8,11},{9,10},{10,... | collective-permute-start | bytes 196616 | tf_op jit(solution)/shard_map/ppermute | solution.py:275
  111.5 9.0 %copy-start.5 = (bf16[2,1,128,128]{3,2,1,0:T(8,128)(2,1)}, bf16[2,1,128,128]{3,2,1,0:T(8,128)(2,1)S(1)}, u32[]{:S(2)}) copy-start(bf16[2,1,128,128]{3,2,1,0:T(8,128)(2,1)S(1)} %get-tuple-element.124.refs_8_) | copy-start | bytes 196612
  111.5 9.6 %collective-permute-start.29 = (bf16[2,1,128,128]{3,2,1,0:T(8,128)(2,1)S(1)}, bf16[2,1,128,128]{3,2,1,0:T(8,128)(2,1)S(1)}, u32[]{:S(2)}, u32[]{:S(2)}) collective-permute-start(bf16[2,1,128,128]{3,2,1,0:T(8,128)(2,1)S(1)} %get-tuple-element.125), channel_id=1, source_target_pairs={{0,1},{1,0},{2,3},{3,2},{4,5},{5,4},{6,7},{7,6},{8,9},{9,8},{10,11... | collective-permute-start | bytes 196616 | tf_op jit(solution)/shard_map/ppermute | solution.py:275
  112.5 8.0 %collective-permute-start.30 = (bf16[2,1,128,128]{3,2,1,0:T(8,128)(2,1)S(1)}, bf16[2,1,128,128]{3,2,1,0:T(8,128)(2,1)S(1)}, u32[]{:S(2)}, u32[]{:S(2)}) collective-permute-start(bf16[2,1,128,128]{3,2,1,0:T(8,128)(2,1)S(1)} %get-tuple-element.126), channel_id=1, source_target_pairs={{0,2},{1,3},{2,0},{3,1},{4,6},{5,7},{6,4},{7,5},{8,10},{9,11},{10,... | collective-permute-start | bytes 196616 | tf_op jit(solution)/shard_map/ppermute | solution.py:275
  114.4 6.1 %collective-permute-start.31 = (bf16[2,1,128,128]{3,2,1,0:T(8,128)(2,1)S(1)}, bf16[2,1,128,128]{3,2,1,0:T(8,128)(2,1)S(1)}, u32[]{:S(2)}, u32[]{:S(2)}) collective-permute-start(bf16[2,1,128,128]{3,2,1,0:T(8,128)(2,1)S(1)} %get-tuple-element.127), channel_id=1, source_target_pairs={{0,3},{1,2},{2,1},{3,0},{4,7},{5,6},{6,5},{7,4},{8,11},{9,10},{10,... | collective-permute-start | bytes 196616 | tf_op jit(solution)/shard_map/ppermute | solution.py:275
  116.0 5.8 %collective-permute-start.32 = (bf16[4,128,128]{2,1,0:T(8,128)(2,1)S(1)}, bf16[4,128,128]{2,1,0:T(8,128)(2,1)S(1)}, u32[]{:S(2)}, u32[]{:S(2)}) collective-permute-start(bf16[4,128,128]{2,1,0:T(8,128)(2,1)S(1)} %pad_maximum_fusion.3), channel_id=1, source_target_pairs={{0,4},{4,0},{8,12},{12,8},{16,20},{20,16},{24,28},{28,24},{1,5},{5... | collective-permute-start | bytes 393224 | tf_op jit(solution)/shard_map/ppermute | solution.py:278
  116.0 5.8 %collective-permute-start.33 = (bf16[4,128,128]{2,1,0:T(8,128)(2,1)S(1)}, bf16[4,128,128]{2,1,0:T(8,128)(2,1)S(1)}, u32[]{:S(2)}, u32[]{:S(2)}) collective-permute-start(bf16[4,128,128]{2,1,0:T(8,128)(2,1)S(1)} %pad_maximum_fusion.4), channel_id=1, source_target_pairs={{0,4},{4,0},{8,12},{12,8},{16,20},{20,16},{24,28},{28,24},{1,5},{5... | collective-permute-start | bytes 393224 | tf_op jit(solution)/shard_map/ppermute | solution.py:278
  121.1 0.6 copy-start.21
  121.8 1.3 %collective-permute-start.34 = (bf16[4,128,128]{2,1,0:T(8,128)(2,1)S(1)}, bf16[4,128,128]{2,1,0:T(8,128)(2,1)S(1)}, u32[]{:S(2)}, u32[]{:S(2)}) collective-permute-start(bf16[4,128,128]{2,1,0:T(8,128)(2,1)S(1)} %pad_maximum_fusion.5), channel_id=1, source_target_pairs={{0,4},{4,0},{8,12},{12,8},{16,20},{20,16},{24,28},{28,24},{1,5},{5... | collective-permute-start | bytes 393224 | tf_op jit(solution)/shard_map/ppermute | solution.py:278
  121.8 1.3 %copy-start.25 = (bf16[4,128,128]{2,1,0:T(8,128)(2,1)}, bf16[4,128,128]{2,1,0:T(8,128)(2,1)S(1)}, u32[]{:S(2)}) copy-start(bf16[4,128,128]{2,1,0:T(8,128)(2,1)S(1)} %collective-permute-done.32.refs_12_) | copy-start | bytes 393220
  121.8 1.3 %copy-start.26 = (bf16[4,128,128]{2,1,0:T(8,128)(2,1)}, bf16[4,128,128]{2,1,0:T(8,128)(2,1)S(1)}, u32[]{:S(2)}) copy-start(bf16[4,128,128]{2,1,0:T(8,128)(2,1)S(1)} %collective-permute-done.33.refs_13_) | copy-start | bytes 393220
  123.1 0.7 copy-start.27
  (5 other events, 3.1 us)

commit v2 on v1

--- a/solution.py
+++ b/solution.py
@@ -10,8 +10,8 @@
 HEAD_DIM = 128
 BLOCK = 128
 EXP2_SCALE = math.log2(math.e) / math.sqrt(HEAD_DIM)
-KERNEL_VMEM = 32 * 2**20
-SCORE_BYTES = 8 * 2**20
+KERNEL_VMEM = 40 * 2**20
+SCORE_BYTES = 16 * 2**20
 
 
 def head_lane(place_ref, way, other, turn, shape):
@@ -229,7 +229,7 @@
         out_shape=out_shape,
         compiler_params=pltpu.CompilerParams(vmem_limit_bytes=KERNEL_VMEM),
         cost_estimate=pl.CostEstimate(
-            flops=40 * units * BLOCK * width * HEAD_DIM,
+            flops=20 * units * BLOCK * width * HEAD_DIM,
             bytes_accessed=4 * width * HEAD_DIM,
             transcendentals=units * BLOCK * width,
         ),

time: 127 us -> 125 us (0.984)
  transfers between devices with their start and end apart: 35 -> 35, of which waited for: 7 -> 7; matrix products, arithmetic and copies ran while one was open for 1% -> 1% of each run, Pallas kernels for 25% -> 24%
where the time goes in v2:
time: 125 us
  starting transfers between devices  45 us (36%)
  Pallas kernels  41.1 us (33%)
  waiting for transfers between devices  30.8 us (25%)
  local copies, waits for them, and re-layouts  5.7 us (5%)
    ppermute x18, starting transfers between devices, swap(): return lax.ppermute(array, 'head', [(z, z ^ way) for z in range(ways)])  31 us
    pallas_call x4, Pallas kernels, attend(): pl.pallas_call(body, grid_spec=pltpu.PrefetchScalarGridSpec(num_scalar_pr...  28 us
    ppermute x18, waiting for transfers between devices, swap(): return lax.ppermute(array, 'head', [(z, z ^ way) for z in range(ways)])  21.9 us
    ppermute x17, starting transfers between devices, send(): return lax.ppermute(array, 'seq', pairs)  14 us
    pallas_call x5, Pallas kernels, in_vmem(): pl.pallas_call(body, in_specs=[pl.BlockSpec(memory_space=pltpu.SMEM)] + [...  13 us
    ppermute x17, waiting for transfers between devices, send(): return lax.ppermute(array, 'seq', pairs)  8.95 us
    unnamed x68, local copies, waits for them, and re-layouts  5.12 us
  transfers between devices with their start and end apart: 35, of which 7 were waited for; matrix products, arithmetic and copies ran while one was open for 1% of the time, Pallas kernels for 24%

profile of v2, /device:TPU:0, one launch (start us, length us, event | category | flops | bytes accessed | tf_op | source)
XLA Modules:
  0.0 124.5 jit_solution(10033667539833625495)
XLA Ops:
  0.0 0.6 pad_add_fusion.place_ref
  0.6 2.2 %pack_twin.3 = bf16[4,2,128,128]{3,2,1,0:T(8,128)(2,1)} custom-call(s32[2]{0:T(128)} %pad_add_fusion.place_ref, bf16[128,3072]{1,0:T(8,128)(2,1)} %refs_0_.7, bf16[128,3072]{1,0:T(8,128)(2,1)} %refs_1_.7), custom_call_target="tpu_custom_call" | custom-call | tf_op jit(solution)/shard_map/pack_twin/pallas_call | solution.py:25
  2.8 0.5 collective-permute-start
  3.3 2.8 %pack_twin.2 = bf16[4,7,128,128]{3,2,1,0:T(8,128)(2,1)} custom-call(s32[2]{0:T(128)} %pad_add_fusion.place_ref, bf16[128,3072]{1,0:T(8,128)(2,1)} %refs_0_.7, bf16[128,3072]{1,0:T(8,128)(2,1)} %refs_1_.7, bf16[128,3072]{1,0:T(8,128)(2,1)} %refs_2_.3), custom_call_target="tpu_custom_call" | custom-call | tf_op jit(solution)/shard_map/pack_twin/pallas_call | solution.py:25
  6.1 0.7 copy-done.17
  6.8 2.3 %pack.2 = (bf16[2,2,128,128]{3,2,1,0:T(8,128)(2,1)}, bf16[2,2,128,128]{3,2,1,0:T(8,128)(2,1)}, bf16[2,2,128,128]{3,2,1,0:T(8,128)(2,1)}, bf16[2,2,128,128]{3,2,1,0:T(8,128)(2,1)}) custom-call(s32[2]{0:T(128)} %pad_add_fusion.place_ref, bf16[128,3072]{1,0:T(8,128)(2,1)} %refs_0_.7, bf16[128,3072]{1,0:T(8,128)(2,1)} %refs_1_.7, bf16[4,2,128,128]{3,2,1,0:T(8,128)(2,1)} %copy-done.17), custom_call_target="tpu_custom_call" | custom-call | tf_op jit(solution)/shard_map/pack/pallas_call | solution.py:25
  9.2 0.1 add.86
  9.3 0.1 add_multiply_fusion.1
  9.3 3.0 %collective-permute-start.2 = (bf16[2,2,128,128]{3,2,1,0:T(8,128)(2,1)}, bf16[2,2,128,128]{3,2,1,0:T(8,128)(2,1)S(1)}, u32[]{:S(2)}, u32[]{:S(2)}) collective-permute-start(bf16[2,2,128,128]{3,2,1,0:T(8,128)(2,1)} %get-tuple-element.72), channel_id=1, source_target_pairs={{0,1},{1,0},{2,3},{3,2},{4,5},{5,4},{6,7},{7,6},{8,9},{9,8},{10,11... | collective-permute-start | bytes 393224 | tf_op jit(solution)/shard_map/ppermute | solution.py:275
  12.4 2.6 %collective-permute-start.4 = (bf16[2,2,128,128]{3,2,1,0:T(8,128)(2,1)}, bf16[2,2,128,128]{3,2,1,0:T(8,128)(2,1)S(1)}, u32[]{:S(2)}, u32[]{:S(2)}) collective-permute-start(bf16[2,2,128,128]{3,2,1,0:T(8,128)(2,1)} %get-tuple-element.75), channel_id=1, source_target_pairs={{0,2},{1,3},{2,0},{3,1},{4,6},{5,7},{6,4},{7,5},{8,10},{9,11},{10,... | collective-permute-start | bytes 393224 | tf_op jit(solution)/shard_map/ppermute | solution.py:275
  14.9 0.1 add_multiply_fusion
  15.0 1.0 copy-done.15
  16.0 3.2 %pack.3 = (bf16[2,3,128,128]{3,2,1,0:T(8,128)(2,1)}, bf16[2,3,128,128]{3,2,1,0:T(8,128)(2,1)}, bf16[2,3,128,128]{3,2,1,0:T(8,128)(2,1)}, bf16[2,3,128,128]{3,2,1...) custom-call(s32[2]{0:T(128)} %pad_add_fusion.place_ref, ...), custom_call_target="tpu_custom_call" | custom-call | tf_op jit(solution)/shard_map/pack/pallas_call | solution.py:25
  19.3 6.2 %collective-permute-done.4 = bf16[2,2,128,128]{3,2,1,0:T(8,128)(2,1)S(1)} collective-permute-done((bf16[2,2,128,128]{3,2,1,0:T(8,128)(2,1)}, bf16[2,2,128,128]{3,2,1,0:T(8,128)(2,1)S(1)}, u32[]{:S(2)}, u32[]{:S(2)}) %collective-permute-start.4) | collective-permute-done | bytes 131104 | tf_op jit(solution)/shard_map/ppermute | solution.py:275
  25.5 0.1 pad_maximum_fusion
  25.6 1.6 %collective-permute-start.8 = (bf16[4,2,2,128,128]{4,3,2,1,0:T(8,128)(2,1)S(1)}, bf16[4,2,2,128,128]{4,3,2,1,0:T(8,128)(2,1)S(1)}, u32[]{:S(2)}, u32[]{:S(2)}) collective-permute-start(bf16[4,2,2,128,128]{4,3,2,1,0:T(8,128)(2,1)S(1)} %get-tuple-element.135), channel_id=1, source_target_pairs={{0,8},{4,20},{8,0},{12,28},{16,24},{20,4},{24,16},{28,12},{1,9},{5... | collective-permute-start | bytes 1572872 | tf_op jit(solution)/shard_map/ppermute | solution.py:278
  27.2 1.5 %collective-permute-start.9 = (bf16[4,2,2,128,128]{4,3,2,1,0:T(8,128)(2,1)S(1)}, bf16[4,2,2,128,128]{4,3,2,1,0:T(8,128)(2,1)S(1)}, u32[]{:S(2)}, u32[]{:S(2)}) collective-permute-start(bf16[4,2,2,128,128]{4,3,2,1,0:T(8,128)(2,1)S(1)} %get-tuple-element.135), channel_id=1, source_target_pairs={{0,16},{4,12},{8,24},{12,4},{16,0},{20,28},{24,8},{28,20},{1,17},{... | collective-permute-start | bytes 1572872 | tf_op jit(solution)/shard_map/ppermute | solution.py:278
  28.7 0.1 add.87
  28.8 0.1 add.88
  28.8 2.4 %collective-permute-start.7 = (bf16[2,3,128,128]{3,2,1,0:T(8,128)(2,1)S(1)}, bf16[2,3,128,128]{3,2,1,0:T(8,128)(2,1)S(1)}, u32[]{:S(2)}, u32[]{:S(2)}) collective-permute-start(bf16[2,3,128,128]{3,2,1,0:T(8,128)(2,1)S(1)} %copy-done.33), channel_id=1, source_target_pairs={{0,3},{1,2},{2,1},{3,0},{4,7},{5,6},{6,5},{7,4},{8,11},{9,10},{10,... | collective-permute-start | bytes 589832 | tf_op jit(solution)/shard_map/ppermute | solution.py:275
  31.3 0.1 broadcast_add_fusion
  31.3 0.1 add.97.key_ids_ref
  31.4 1.4 %collective-permute-start.3 = (bf16[2,3,128,128]{3,2,1,0:T(8,128)(2,1)S(1)}, bf16[2,3,128,128]{3,2,1,0:T(8,128)(2,1)S(1)}, u32[]{:S(2)}, u32[]{:S(2)}) collective-permute-start(bf16[2,3,128,128]{3,2,1,0:T(8,128)(2,1)S(1)} %copy-done.31), channel_id=1, source_target_pairs={{0,1},{1,0},{2,3},{3,2},{4,5},{5,4},{6,7},{7,6},{8,9},{9,8},{10,11... | collective-permute-start | bytes 589832 | tf_op jit(solution)/shard_map/ppermute | solution.py:275
  32.8 0.7 collective-permute-start.5
  33.5 5.1 %collective-permute-done.7.refs_3_ = bf16[2,3,128,128]{3,2,1,0:T(8,128)(2,1)S(1)} collective-permute-done((bf16[2,3,128,128]{3,2,1,0:T(8,128)(2,1)S(1)}, bf16[2,3,128,128]{3,2,1,0:T(8,128)(2,1)S(1)}, u32[]{:S(2)}, u32[]{:S(2)}) %collective-permute-start.7) | collective-permute-done | bytes 196640 | tf_op jit(solution)/shard_map/ppermute | solution.py:275
  38.7 0.7 collective-permute-start.10
  39.3 1.5 %collective-permute-start.11 = (bf16[2,2,2,128,128]{4,3,2,1,0:T(8,128)(2,1)S(1)}, bf16[2,2,2,128,128]{4,3,2,1,0:T(8,128)(2,1)S(1)}, u32[]{:S(2)}, u32[]{:S(2)}) collective-permute-start(bf16[2,2,2,128,128]{4,3,2,1,0:T(8,128)(2,1)S(1)} %slice.105), channel_id=1, source_target_pairs={{0,8},{4,20},{8,0},{12,28},{16,24},{20,4},{24,16},{28,12},{1,9},{5... | collective-permute-start | bytes 786440 | tf_op jit(solution)/shard_map/ppermute | solution.py:278
  40.8 6.5 %collective-permute-done.5.refs_2_ = bf16[2,3,128,128]{3,2,1,0:T(8,128)(2,1)S(1)} collective-permute-done((bf16[2,3,128,128]{3,2,1,0:T(8,128)(2,1)S(1)}, bf16[2,3,128,128]{3,2,1,0:T(8,128)(2,1)S(1)}, u32[]{:S(2)}, u32[]{:S(2)}) %collective-permute-start.5) | collective-permute-done | bytes 196640 | tf_op jit(solution)/shard_map/ppermute | solution.py:275
  47.4 0.9 copy-done.7
  48.4 0.1 fusion.1
  48.5 0.6 collective-permute-start.12
  49.1 0.6 collective-permute-start.13
  49.7 2.5 %collective-permute-start.18 = (bf16[2,3,128,128]{3,2,1,0:T(8,128)(2,1)S(1)}, bf16[2,3,128,128]{3,2,1,0:T(8,128)(2,1)S(1)}, u32[]{:S(2)}, u32[]{:S(2)}) collective-permute-start(bf16[2,3,128,128]{3,2,1,0:T(8,128)(2,1)S(1)} %copy-done.30), channel_id=1, source_target_pairs={{0,3},{1,2},{2,1},{3,0},{4,7},{5,6},{6,5},{7,4},{8,11},{9,10},{10,... | collective-permute-start | bytes 589832 | tf_op jit(solution)/shard_map/ppermute | solution.py:275
  52.1 5.3 %collective-permute-start.17 = (bf16[2,3,128,128]{3,2,1,0:T(8,128)(2,1)S(1)}, bf16[2,3,128,128]{3,2,1,0:T(8,128)(2,1)S(1)}, u32[]{:S(2)}, u32[]{:S(2)}) collective-permute-start(bf16[2,3,128,128]{3,2,1,0:T(8,128)(2,1)S(1)} %copy-done.29), channel_id=1, source_target_pairs={{0,2},{1,3},{2,0},{3,1},{4,6},{5,7},{6,4},{7,5},{8,10},{9,11},{10,... | collective-permute-start | bytes 589832 | tf_op jit(solution)/shard_map/ppermute | solution.py:275
  57.5 0.6 copy-done.8
  58.1 9.0 %attend.4 = (bf16[2,2,128,128]{3,2,1,0:T(8,128)(2,1)S(1)}, bf16[2,2,128,128]{3,2,1,0:T(8,128)(2,1)S(1)}, bf16[2,2,128,128]{3,2,1,0:T(8,128)(2,1)S(1)}, bf16[2,2,128,128]{3,2,1,0:T(8,128)(2,1)S(1)}) custom-call(s32[2]{0:T(128)S(1)} %copy-done.8, s32[32]{0:T(128)S(1)} %copy-done.14, s32[8]{0:T(128)S(1)} %add.89.query_ids_ref, s32[32]{0:T(128)S(1)} %add.97.key_ids_ref, ...), custom_call_target="tpu_custom_call" | custom-call | flops 10737418240 | bytes 2097152 | tf_op jit(solution)/shard_map/attend/pallas_call | solution.py:209
  67.2 0.7 collective-permute-start.14
  67.9 1.5 %collective-permute-start.15 = (bf16[2,2,2,128,128]{4,3,2,1,0:T(8,128)(2,1)S(1)}, bf16[2,2,2,128,128]{4,3,2,1,0:T(8,128)(2,1)S(1)}, u32[]{:S(2)}, u32[]{:S(2)}) collective-permute-start(bf16[2,2,2,128,128]{4,3,2,1,0:T(8,128)(2,1)S(1)} %slice.110), channel_id=1, source_target_pairs={{0,8},{4,20},{8,0},{12,28},{16,24},{20,4},{24,16},{28,12},{1,9},{5... | collective-permute-start | bytes 786440 | tf_op jit(solution)/shard_map/ppermute | solution.py:278
  69.5 6.9 %collective-permute-done.14 = bf16[2,2,2,128,128]{4,3,2,1,0:T(8,128)(2,1)S(1)} collective-permute-done((bf16[2,2,2,128,128]{4,3,2,1,0:T(8,128)(2,1)S(1)}, bf16[2,2,2,128,128]{4,3,2,1,0:T(8,128)(2,1)S(1)}, u32[]{:S(2)}, u32[]{:S(2)}) %collective-permute-start.14) | collective-permute-done | bytes 262176 | tf_op jit(solution)/shard_map/ppermute | solution.py:278
  76.3 0.7 collective-permute-done.15
  77.1 0.1 fusion
  77.2 1.5 %collective-permute-start.22 = (bf16[4,2,2,128,128]{4,3,2,1,0:T(8,128)(2,1)S(1)}, bf16[4,2,2,128,128]{4,3,2,1,0:T(8,128)(2,1)S(1)}, u32[]{:S(2)}, u32[]{:S(2)}) collective-permute-start(bf16[4,2,2,128,128]{4,3,2,1,0:T(8,128)(2,1)S(1)} %get-tuple-element.132), channel_id=1, source_target_pairs={{0,8},{4,20},{8,0},{12,28},{16,24},{20,4},{24,16},{28,12},{1,9},{5... | collective-permute-start | bytes 1572872 | tf_op jit(solution)/shard_map/ppermute | solution.py:278
  78.7 1.4 %collective-permute-start.23 = (bf16[4,2,2,128,128]{4,3,2,1,0:T(8,128)(2,1)S(1)}, bf16[4,2,2,128,128]{4,3,2,1,0:T(8,128)(2,1)S(1)}, u32[]{:S(2)}, u32[]{:S(2)}) collective-permute-start(bf16[4,2,2,128,128]{4,3,2,1,0:T(8,128)(2,1)S(1)} %get-tuple-element.132), channel_id=1, source_target_pairs={{0,16},{4,12},{8,24},{12,4},{16,0},{20,28},{24,8},{28,20},{1,17},{... | collective-permute-start | bytes 1572872 | tf_op jit(solution)/shard_map/ppermute | solution.py:278
  80.2 1.6 %collective-permute-start.19 = (bf16[2,2,128,128]{3,2,1,0:T(8,128)(2,1)S(1)}, bf16[2,2,128,128]{3,2,1,0:T(8,128)(2,1)S(1)}, u32[]{:S(2)}, u32[]{:S(2)}) collective-permute-start(bf16[2,2,128,128]{3,2,1,0:T(8,128)(2,1)S(1)} %get-tuple-element.107), channel_id=1, source_target_pairs={{0,1},{1,0},{2,3},{3,2},{4,5},{5,4},{6,7},{7,6},{8,9},{9,8},{10,11... | collective-permute-start | bytes 393224 | tf_op jit(solution)/shard_map/ppermute | solution.py:275
  81.8 1.2 collective-permute-start.20
  83.0 1.6 %collective-permute-start.21 = (bf16[2,2,128,128]{3,2,1,0:T(8,128)(2,1)S(1)}, bf16[2,2,128,128]{3,2,1,0:T(8,128)(2,1)S(1)}, u32[]{:S(2)}, u32[]{:S(2)}) collective-permute-start(bf16[2,2,128,128]{3,2,1,0:T(8,128)(2,1)S(1)} %get-tuple-element.109), channel_id=1, source_target_pairs={{0,3},{1,2},{2,1},{3,0},{4,7},{5,6},{6,5},{7,4},{8,11},{9,10},{10,... | collective-permute-start | bytes 393224 | tf_op jit(solution)/shard_map/ppermute | solution.py:275
  84.5 9.2 %attend.5 = (bf16[2,1,128,128]{3,2,1,0:T(8,128)(2,1)S(1)}, bf16[2,1,128,128]{3,2,1,0:T(8,128)(2,1)S(1)}, bf16[2,1,128,128]{3,2,1,0:T(8,128)(2,1)S(1)}, bf16[2,1,128,128]{3,2,1,0:T(8,128)(2,1)S(1)}) custom-call(s32[2]{0:T(128)S(1)} %copy-done.8, s32[32]{0:T(128)S(1)} %copy-done.14, s32[8]{0:T(128)S(1)} %add.89.query_ids_ref, s32[32]{0:T(128)S(1)} %add.97.key_ids_ref, ...), custom_call_target="tpu_custom_call" | custom-call | flops 10737418240 | bytes 2097152 | tf_op jit(solution)/shard_map/attend/pallas_call | solution.py:209
  94.0 0.8 collective-permute-start.27
  94.8 0.5 collective-permute-start.28
  95.3 1.8 %collective-permute-start.24 = (bf16[2,1,128,128]{3,2,1,0:T(8,128)(2,1)S(1)}, bf16[2,1,128,128]{3,2,1,0:T(8,128)(2,1)S(1)}, u32[]{:S(2)}, u32[]{:S(2)}) collective-permute-start(bf16[2,1,128,128]{3,2,1,0:T(8,128)(2,1)S(1)} %get-tuple-element.118), channel_id=1, source_target_pairs={{0,1},{1,0},{2,3},{3,2},{4,5},{5,4},{6,7},{7,6},{8,9},{9,8},{10,11... | collective-permute-start | bytes 196616 | tf_op jit(solution)/shard_map/ppermute | solution.py:275
  97.1 1.1 collective-permute-start.25
  98.1 1.5 %collective-permute-start.26 = (bf16[2,1,128,128]{3,2,1,0:T(8,128)(2,1)S(1)}, bf16[2,1,128,128]{3,2,1,0:T(8,128)(2,1)S(1)}, u32[]{:S(2)}, u32[]{:S(2)}) collective-permute-start(bf16[2,1,128,128]{3,2,1,0:T(8,128)(2,1)S(1)} %get-tuple-element.120), channel_id=1, source_target_pairs={{0,3},{1,2},{2,1},{3,0},{4,7},{5,6},{6,5},{7,4},{8,11},{9,10},{10,... | collective-permute-start | bytes 196616 | tf_op jit(solution)/shard_map/ppermute | solution.py:275
  99.7 6.0 %attend.6 = (f32[1024,128]{1,0:T(8,128)S(1)}, f32[1024,128]{1,0:T(8,128)S(1)}, f32[1024,128]{1,0:T(8,128)S(1)}) custom-call(s32[2]{0:T(128)S(1)} %copy-done.8, s32[32]{0:T(128)S(1)} %copy-done.14, s32[8]{0:T(128)S(1)} %add.89.query_ids_ref, s32[32]{0:T(128)S(1)} %add.97.key_ids_ref, s32[6,32,32]{2,1,0:T(8,128)S(1)} %copy-done.9, ...), custom_call_target="tpu_custom_call" | custom-call | flops 8053063680 | bytes 1572864 | tf_op jit(solution)/shard_map/attend/pallas_call | solution.py:209
  105.8 0.5 copy-done.20
  106.5 3.8 %attend.7 = (bf16[2,1,128,128]{3,2,1,0:T(8,128)(2,1)S(1)}, bf16[2,1,128,128]{3,2,1,0:T(8,128)(2,1)S(1)}, bf16[2,1,128,128]{3,2,1,0:T(8,128)(2,1)S(1)}, bf16[2,1,128,128]{3,2,1,0:T(8,128)(2,1)S(1)}) custom-call(s32[2]{0:T(128)S(1)} %copy-done.8, s32[32]{0:T(128)S(1)} %copy-done.14, s32[8]{0:T(128)S(1)} %add.89.query_ids_ref, s32[32]{0:T(128)S(1)} %add.97.key_ids_ref, ...), custom_call_target="tpu_custom_call" | custom-call | flops 2684354560 | bytes 524288 | tf_op jit(solution)/shard_map/attend/pallas_call | solution.py:209
  110.3 1.7 %collective-permute-start.29 = (bf16[2,1,128,128]{3,2,1,0:T(8,128)(2,1)S(1)}, bf16[2,1,128,128]{3,2,1,0:T(8,128)(2,1)S(1)}, u32[]{:S(2)}, u32[]{:S(2)}) collective-permute-start(bf16[2,1,128,128]{3,2,1,0:T(8,128)(2,1)S(1)} %get-tuple-element.125), channel_id=1, source_target_pairs={{0,1},{1,0},{2,3},{3,2},{4,5},{5,4},{6,7},{7,6},{8,9},{9,8},{10,11... | collective-permute-start | bytes 196616 | tf_op jit(solution)/shard_map/ppermute | solution.py:275
  111.9 1.3 %collective-permute-start.30 = (bf16[2,1,128,128]{3,2,1,0:T(8,128)(2,1)S(1)}, bf16[2,1,128,128]{3,2,1,0:T(8,128)(2,1)S(1)}, u32[]{:S(2)}, u32[]{:S(2)}) collective-permute-start(bf16[2,1,128,128]{3,2,1,0:T(8,128)(2,1)S(1)} %get-tuple-element.126), channel_id=1, source_target_pairs={{0,2},{1,3},{2,0},{3,1},{4,6},{5,7},{6,4},{7,5},{8,10},{9,11},{10,... | collective-permute-start | bytes 196616 | tf_op jit(solution)/shard_map/ppermute | solution.py:275
  113.2 1.5 %collective-permute-start.31 = (bf16[2,1,128,128]{3,2,1,0:T(8,128)(2,1)S(1)}, bf16[2,1,128,128]{3,2,1,0:T(8,128)(2,1)S(1)}, u32[]{:S(2)}, u32[]{:S(2)}) collective-permute-start(bf16[2,1,128,128]{3,2,1,0:T(8,128)(2,1)S(1)} %get-tuple-element.127), channel_id=1, source_target_pairs={{0,3},{1,2},{2,1},{3,0},{4,7},{5,6},{6,5},{7,4},{8,11},{9,10},{10,... | collective-permute-start | bytes 196616 | tf_op jit(solution)/shard_map/ppermute | solution.py:275
  114.7 0.5 collective-permute-start.33
  115.2 4.0 %collective-permute-done.31.refs_11_ = bf16[2,1,128,128]{3,2,1,0:T(8,128)(2,1)S(1)} collective-permute-done((bf16[2,1,128,128]{3,2,1,0:T(8,128)(2,1)S(1)}, bf16[2,1,128,128]{3,2,1,0:T(8,128)(2,1)S(1)}, u32[]{:S(2)}, u32[]{:S(2)}) %collective-permute-start.31) | collective-permute-done | bytes 65568 | tf_op jit(solution)/shard_map/ppermute | solution.py:275
  119.3 0.6 copy-done.23
  120.1 1.3 %collective-permute-done.34.refs_14_ = bf16[4,128,128]{2,1,0:T(8,128)(2,1)S(1)} collective-permute-done((bf16[4,128,128]{2,1,0:T(8,128)(2,1)S(1)}, bf16[4,128,128]{2,1,0:T(8,128)(2,1)S(1)}, u32[]{:S(2)}, u32[]{:S(2)}) %collective-permute-start.34) | collective-permute-done | bytes 131104 | tf_op jit(solution)/shard_map/ppermute | solution.py:278
  121.4 0.7 copy-done.27
  122.0 2.5 %unpack.1 = bf16[128,3072]{1,0:T(8,128)(2,1)} custom-call(s32[2]{0:T(128)} %pad_add_fusion.place_ref, bf16[2,2,128,128]{3,2,1,0:T(8,128)(2,1)} %copy-done, bf16[2,2,128,128]{3,2,1,0:T(8,128)(2,1)} %copy-done.1, bf16[2,2,128,128]{3,2,1,0:T(8,128)(2,1)} %copy-done.2, bf16[2,2,128,128]{3,2,1,0:T(8,128)(2,1)} %copy-done.3, bf16[2,1,128,128]{3,2,1,0:T(8,128)(2,1)} %copy-done.4, ...), custom_call_target="tpu_custom_call" | custom-call | tf_op jit(solution)/shard_map/unpack/pallas_call | solution.py:25
  (127 shorter events, 0.7 us)
Async XLA Ops:
  2.8 3.3 %collective-permute-start = (bf16[4,2,128,128]{3,2,1,0:T(8,128)(2,1)}, bf16[4,2,128,128]{3,2,1,0:T(8,128)(2,1)S(1)}, u32[]{:S(2)}, u32[]{:S(2)}) collective-permute-start(bf16[4,2,128,128]{3,2,1,0:T(8,128)(2,1)} %pack_twin.3), channel_id=1, source_target_pairs={{0,4},{4,0},{8,12},{12,8},{16,20},{20,16},{24,28},{28,24},{1,5},{5... | collective-permute-start | bytes 786440 | tf_op jit(solution)/shard_map/ppermute | solution.py:278
  6.1 3.0 %copy-start.16 = (bf16[4,7,128,128]{3,2,1,0:T(8,128)(2,1)S(1)}, bf16[4,7,128,128]{3,2,1,0:T(8,128)(2,1)}, u32[]{:S(2)}) copy-start(bf16[4,7,128,128]{3,2,1,0:T(8,128)(2,1)} %pack_twin.2) | copy-start | bytes 2752516
  6.1 0.7 copy-start.17
  9.1 5.9 %collective-permute-start.1 = (bf16[4,7,128,128]{3,2,1,0:T(8,128)(2,1)S(1)}, bf16[4,7,128,128]{3,2,1,0:T(8,128)(2,1)S(1)}, u32[]{:S(2)}, u32[]{:S(2)}) collective-permute-start(bf16[4,7,128,128]{3,2,1,0:T(8,128)(2,1)S(1)} %copy-done.16), channel_id=1, source_target_pairs={{0,4},{4,0},{8,12},{12,8},{16,20},{20,16},{24,28},{28,24},{1,5},{5... | collective-permute-start | bytes 2752520 | tf_op jit(solution)/shard_map/ppermute | solution.py:278
  9.3 9.9 %collective-permute-start.2 = (bf16[2,2,128,128]{3,2,1,0:T(8,128)(2,1)}, bf16[2,2,128,128]{3,2,1,0:T(8,128)(2,1)S(1)}, u32[]{:S(2)}, u32[]{:S(2)}) collective-permute-start(bf16[2,2,128,128]{3,2,1,0:T(8,128)(2,1)} %get-tuple-element.72), channel_id=1, source_target_pairs={{0,1},{1,0},{2,3},{3,2},{4,5},{5,4},{6,7},{7,6},{8,9},{9,8},{10,11... | collective-permute-start | bytes 393224 | tf_op jit(solution)/shard_map/ppermute | solution.py:275
  12.4 13.1 %collective-permute-start.4 = (bf16[2,2,128,128]{3,2,1,0:T(8,128)(2,1)}, bf16[2,2,128,128]{3,2,1,0:T(8,128)(2,1)S(1)}, u32[]{:S(2)}, u32[]{:S(2)}) collective-permute-start(bf16[2,2,128,128]{3,2,1,0:T(8,128)(2,1)} %get-tuple-element.75), channel_id=1, source_target_pairs={{0,2},{1,3},{2,0},{3,1},{4,6},{5,7},{6,4},{7,5},{8,10},{9,11},{10,... | collective-permute-start | bytes 393224 | tf_op jit(solution)/shard_map/ppermute | solution.py:275
  14.9 10.5 %collective-permute-start.6 = (bf16[2,2,128,128]{3,2,1,0:T(8,128)(2,1)}, bf16[2,2,128,128]{3,2,1,0:T(8,128)(2,1)S(1)}, u32[]{:S(2)}, u32[]{:S(2)}) collective-permute-start(bf16[2,2,128,128]{3,2,1,0:T(8,128)(2,1)} %get-tuple-element.78), channel_id=1, source_target_pairs={{0,3},{1,2},{2,1},{3,0},{4,7},{5,6},{6,5},{7,4},{8,11},{9,10},{10,... | collective-permute-start | bytes 393224 | tf_op jit(solution)/shard_map/ppermute | solution.py:275
  15.0 10.5 %copy-start.24 = (bf16[2,2,128,128]{3,2,1,0:T(8,128)(2,1)S(1)}, bf16[2,2,128,128]{3,2,1,0:T(8,128)(2,1)}, u32[]{:S(2)}) copy-start(bf16[2,2,128,128]{3,2,1,0:T(8,128)(2,1)} %get-tuple-element.80) | copy-start | bytes 393220
  15.0 1.0 copy-start.15
  25.5 3.4 %copy-start.33 = (bf16[2,3,128,128]{3,2,1,0:T(8,128)(2,1)S(1)}, bf16[2,3,128,128]{3,2,1,0:T(8,128)(2,1)}, u32[]{:S(2)}) copy-start(bf16[2,3,128,128]{3,2,1,0:T(8,128)(2,1)} %get-tuple-element.79) | copy-start | bytes 589828
  25.5 5.9 %copy-start.31 = (bf16[2,3,128,128]{3,2,1,0:T(8,128)(2,1)S(1)}, bf16[2,3,128,128]{3,2,1,0:T(8,128)(2,1)}, u32[]{:S(2)}) copy-start(bf16[2,3,128,128]{3,2,1,0:T(8,128)(2,1)} %get-tuple-element.73) | copy-start | bytes 589828
  25.5 7.3 %copy-start.32 = (bf16[2,3,128,128]{3,2,1,0:T(8,128)(2,1)S(1)}, bf16[2,3,128,128]{3,2,1,0:T(8,128)(2,1)}, u32[]{:S(2)}) copy-start(bf16[2,3,128,128]{3,2,1,0:T(8,128)(2,1)} %get-tuple-element.76) | copy-start | bytes 589828
  25.6 13.0 %collective-permute-start.8 = (bf16[4,2,2,128,128]{4,3,2,1,0:T(8,128)(2,1)S(1)}, bf16[4,2,2,128,128]{4,3,2,1,0:T(8,128)(2,1)S(1)}, u32[]{:S(2)}, u32[]{:S(2)}) collective-permute-start(bf16[4,2,2,128,128]{4,3,2,1,0:T(8,128)(2,1)S(1)} %get-tuple-element.135), channel_id=1, source_target_pairs={{0,8},{4,20},{8,0},{12,28},{16,24},{20,4},{24,16},{28,12},{1,9},{5... | collective-permute-start | bytes 1572872 | tf_op jit(solution)/shard_map/ppermute | solution.py:278
  27.2 11.5 %collective-permute-start.9 = (bf16[4,2,2,128,128]{4,3,2,1,0:T(8,128)(2,1)S(1)}, bf16[4,2,2,128,128]{4,3,2,1,0:T(8,128)(2,1)S(1)}, u32[]{:S(2)}, u32[]{:S(2)}) collective-permute-start(bf16[4,2,2,128,128]{4,3,2,1,0:T(8,128)(2,1)S(1)} %get-tuple-element.135), channel_id=1, source_target_pairs={{0,16},{4,12},{8,24},{12,4},{16,0},{20,28},{24,8},{28,20},{1,17},{... | collective-permute-start | bytes 1572872 | tf_op jit(solution)/shard_map/ppermute | solution.py:278
  28.8 9.7 %collective-permute-start.7 = (bf16[2,3,128,128]{3,2,1,0:T(8,128)(2,1)S(1)}, bf16[2,3,128,128]{3,2,1,0:T(8,128)(2,1)S(1)}, u32[]{:S(2)}, u32[]{:S(2)}) collective-permute-start(bf16[2,3,128,128]{3,2,1,0:T(8,128)(2,1)S(1)} %copy-done.33), channel_id=1, source_target_pairs={{0,3},{1,2},{2,1},{3,0},{4,7},{5,6},{6,5},{7,4},{8,11},{9,10},{10,... | collective-permute-start | bytes 589832 | tf_op jit(solution)/shard_map/ppermute | solution.py:275
  31.4 15.9 %collective-permute-start.3 = (bf16[2,3,128,128]{3,2,1,0:T(8,128)(2,1)S(1)}, bf16[2,3,128,128]{3,2,1,0:T(8,128)(2,1)S(1)}, u32[]{:S(2)}, u32[]{:S(2)}) collective-permute-start(bf16[2,3,128,128]{3,2,1,0:T(8,128)(2,1)S(1)} %copy-done.31), channel_id=1, source_target_pairs={{0,1},{1,0},{2,3},{3,2},{4,5},{5,4},{6,7},{7,6},{8,9},{9,8},{10,11... | collective-permute-start | bytes 589832 | tf_op jit(solution)/shard_map/ppermute | solution.py:275
  32.8 14.5 %collective-permute-start.5 = (bf16[2,3,128,128]{3,2,1,0:T(8,128)(2,1)S(1)}, bf16[2,3,128,128]{3,2,1,0:T(8,128)(2,1)S(1)}, u32[]{:S(2)}, u32[]{:S(2)}) collective-permute-start(bf16[2,3,128,128]{3,2,1,0:T(8,128)(2,1)S(1)} %copy-done.32), channel_id=1, source_target_pairs={{0,2},{1,3},{2,0},{3,1},{4,6},{5,7},{6,4},{7,5},{8,10},{9,11},{10,... | collective-permute-start | bytes 589832 | tf_op jit(solution)/shard_map/ppermute | solution.py:275
  38.7 8.7 %collective-permute-start.10 = (bf16[2,2,2,128,128]{4,3,2,1,0:T(8,128)(2,1)S(1)}, bf16[2,2,2,128,128]{4,3,2,1,0:T(8,128)(2,1)S(1)}, u32[]{:S(2)}, u32[]{:S(2)}) collective-permute-start(bf16[2,2,2,128,128]{4,3,2,1,0:T(8,128)(2,1)S(1)} %slice.104), channel_id=1, source_target_pairs={{0,16},{4,12},{8,24},{12,4},{16,0},{20,28},{24,8},{28,20},{1,17},{... | collective-permute-start | bytes 786440 | tf_op jit(solution)/shard_map/ppermute | solution.py:278
  39.3 8.1 %collective-permute-start.11 = (bf16[2,2,2,128,128]{4,3,2,1,0:T(8,128)(2,1)S(1)}, bf16[2,2,2,128,128]{4,3,2,1,0:T(8,128)(2,1)S(1)}, u32[]{:S(2)}, u32[]{:S(2)}) collective-permute-start(bf16[2,2,2,128,128]{4,3,2,1,0:T(8,128)(2,1)S(1)} %slice.105), channel_id=1, source_target_pairs={{0,8},{4,20},{8,0},{12,28},{16,24},{20,4},{24,16},{28,12},{1,9},{5... | collective-permute-start | bytes 786440 | tf_op jit(solution)/shard_map/ppermute | solution.py:278
  47.3 0.9 copy-start.7
  48.3 1.4 %copy-start.30 = (bf16[2,3,128,128]{3,2,1,0:T(8,128)(2,1)S(1)}, bf16[2,3,128,128]{3,2,1,0:T(8,128)(2,1)}, u32[]{:S(2)}) copy-start(bf16[2,3,128,128]{3,2,1,0:T(8,128)(2,1)} %get-tuple-element.105) | copy-start | bytes 589828
  48.3 3.8 %copy-start.29 = (bf16[2,3,128,128]{3,2,1,0:T(8,128)(2,1)S(1)}, bf16[2,3,128,128]{3,2,1,0:T(8,128)(2,1)}, u32[]{:S(2)}) copy-start(bf16[2,3,128,128]{3,2,1,0:T(8,128)(2,1)} %get-tuple-element.102) | copy-start | bytes 589828
  48.3 9.1 %copy-start.28 = (bf16[2,3,128,128]{3,2,1,0:T(8,128)(2,1)S(1)}, bf16[2,3,128,128]{3,2,1,0:T(8,128)(2,1)}, u32[]{:S(2)}) copy-start(bf16[2,3,128,128]{3,2,1,0:T(8,128)(2,1)} %get-tuple-element.99) | copy-start | bytes 589828
  48.3 9.1 %copy-start.9 = (s32[6,32,32]{2,1,0:T(8,128)S(1)}, s32[6,32,32]{2,1,0:T(8,128)}, u32[]{:S(2)}) copy-start(s32[6,32,32]{2,1,0:T(8,128)} %mask_ref.7) | copy-start | bytes 73732
  48.3 9.1 %copy-start.10 = (bf16[2,1,128,128]{3,2,1,0:T(8,128)(2,1)S(1)}, bf16[2,1,128,128]{3,2,1,0:T(8,128)(2,1)}, u32[]{:S(2)}) copy-start(bf16[2,1,128,128]{3,2,1,0:T(8,128)(2,1)} %get-tuple-element.85.refs_9_) | copy-start | bytes 196612
  48.3 9.1 %copy-start.11 = (bf16[2,1,128,128]{3,2,1,0:T(8,128)(2,1)S(1)}, bf16[2,1,128,128]{3,2,1,0:T(8,128)(2,1)}, u32[]{:S(2)}) copy-start(bf16[2,1,128,128]{3,2,1,0:T(8,128)(2,1)} %get-tuple-element.86.refs_10_) | copy-start | bytes 196612
  48.4 9.1 %copy-start.12 = (bf16[2,1,128,128]{3,2,1,0:T(8,128)(2,1)S(1)}, bf16[2,1,128,128]{3,2,1,0:T(8,128)(2,1)}, u32[]{:S(2)}) copy-start(bf16[2,1,128,128]{3,2,1,0:T(8,128)(2,1)} %get-tuple-element.87.refs_11_) | copy-start | bytes 196612
  48.4 9.1 %copy-start.13 = (bf16[2,1,128,128]{3,2,1,0:T(8,128)(2,1)S(1)}, bf16[2,1,128,128]{3,2,1,0:T(8,128)(2,1)}, u32[]{:S(2)}) copy-start(bf16[2,1,128,128]{3,2,1,0:T(8,128)(2,1)} %get-tuple-element.88.refs_12_) | copy-start | bytes 196612
  48.5 18.6 %collective-permute-start.12 = (bf16[4,2,2,128,128]{4,3,2,1,0:T(8,128)(2,1)S(1)}, bf16[4,2,2,128,128]{4,3,2,1,0:T(8,128)(2,1)S(1)}, u32[]{:S(2)}, u32[]{:S(2)}) collective-permute-start(bf16[4,2,2,128,128]{4,3,2,1,0:T(8,128)(2,1)S(1)} %get-tuple-element.134), channel_id=1, source_target_pairs={{0,8},{4,20},{8,0},{12,28},{16,24},{20,4},{24,16},{28,12},{1,9},{5... | collective-permute-start | bytes 1572872 | tf_op jit(solution)/shard_map/ppermute | solution.py:278
  49.1 18.1 %collective-permute-start.13 = (bf16[4,2,2,128,128]{4,3,2,1,0:T(8,128)(2,1)S(1)}, bf16[4,2,2,128,128]{4,3,2,1,0:T(8,128)(2,1)S(1)}, u32[]{:S(2)}, u32[]{:S(2)}) collective-permute-start(bf16[4,2,2,128,128]{4,3,2,1,0:T(8,128)(2,1)S(1)} %get-tuple-element.134), channel_id=1, source_target_pairs={{0,16},{4,12},{8,24},{12,4},{16,0},{20,28},{24,8},{28,20},{1,17},{... | collective-permute-start | bytes 1572872 | tf_op jit(solution)/shard_map/ppermute | solution.py:278
  49.7 17.4 %collective-permute-start.18 = (bf16[2,3,128,128]{3,2,1,0:T(8,128)(2,1)S(1)}, bf16[2,3,128,128]{3,2,1,0:T(8,128)(2,1)S(1)}, u32[]{:S(2)}, u32[]{:S(2)}) collective-permute-start(bf16[2,3,128,128]{3,2,1,0:T(8,128)(2,1)S(1)} %copy-done.30), channel_id=1, source_target_pairs={{0,3},{1,2},{2,1},{3,0},{4,7},{5,6},{6,5},{7,4},{8,11},{9,10},{10,... | collective-permute-start | bytes 589832 | tf_op jit(solution)/shard_map/ppermute | solution.py:275
  52.1 17.3 %collective-permute-start.17 = (bf16[2,3,128,128]{3,2,1,0:T(8,128)(2,1)S(1)}, bf16[2,3,128,128]{3,2,1,0:T(8,128)(2,1)S(1)}, u32[]{:S(2)}, u32[]{:S(2)}) collective-permute-start(bf16[2,3,128,128]{3,2,1,0:T(8,128)(2,1)S(1)} %copy-done.29), channel_id=1, source_target_pairs={{0,2},{1,3},{2,0},{3,1},{4,6},{5,7},{6,4},{7,5},{8,10},{9,11},{10,... | collective-permute-start | bytes 589832 | tf_op jit(solution)/shard_map/ppermute | solution.py:275
  57.4 12.0 %collective-permute-start.16 = (bf16[2,3,128,128]{3,2,1,0:T(8,128)(2,1)S(1)}, bf16[2,3,128,128]{3,2,1,0:T(8,128)(2,1)S(1)}, u32[]{:S(2)}, u32[]{:S(2)}) collective-permute-start(bf16[2,3,128,128]{3,2,1,0:T(8,128)(2,1)S(1)} %copy-done.28), channel_id=1, source_target_pairs={{0,1},{1,0},{2,3},{3,2},{4,5},{5,4},{6,7},{7,6},{8,9},{9,8},{10,11... | collective-permute-start | bytes 589832 | tf_op jit(solution)/shard_map/ppermute | solution.py:275
  57.4 0.7 copy-start.8
  57.4 0.7 copy-start.14
  67.1 39.4 %copy-start = (bf16[2,2,128,128]{3,2,1,0:T(8,128)(2,1)}, bf16[2,2,128,128]{3,2,1,0:T(8,128)(2,1)S(1)}, u32[]{:S(2)}) copy-start(bf16[2,2,128,128]{3,2,1,0:T(8,128)(2,1)S(1)} %get-tuple-element.106.refs_0_) | copy-start | bytes 393220
  67.2 9.2 %collective-permute-start.14 = (bf16[2,2,2,128,128]{4,3,2,1,0:T(8,128)(2,1)S(1)}, bf16[2,2,2,128,128]{4,3,2,1,0:T(8,128)(2,1)S(1)}, u32[]{:S(2)}, u32[]{:S(2)}) collective-permute-start(bf16[2,2,2,128,128]{4,3,2,1,0:T(8,128)(2,1)S(1)} %slice.109), channel_id=1, source_target_pairs={{0,16},{4,12},{8,24},{12,4},{16,0},{20,28},{24,8},{28,20},{1,17},{... | collective-permute-start | bytes 786440 | tf_op jit(solution)/shard_map/ppermute | solution.py:278
  67.9 9.2 %collective-permute-start.15 = (bf16[2,2,2,128,128]{4,3,2,1,0:T(8,128)(2,1)S(1)}, bf16[2,2,2,128,128]{4,3,2,1,0:T(8,128)(2,1)S(1)}, u32[]{:S(2)}, u32[]{:S(2)}) collective-permute-start(bf16[2,2,2,128,128]{4,3,2,1,0:T(8,128)(2,1)S(1)} %slice.110), channel_id=1, source_target_pairs={{0,8},{4,20},{8,0},{12,28},{16,24},{20,4},{24,16},{28,12},{1,9},{5... | collective-permute-start | bytes 786440 | tf_op jit(solution)/shard_map/ppermute | solution.py:278
  69.4 7.7 %copy-start.6 = (bf16[2,3,128,128]{3,2,1,0:T(8,128)(2,1)S(1)}, bf16[2,3,128,128]{3,2,1,0:T(8,128)(2,1)}, u32[]{:S(2)}) copy-start(bf16[2,3,128,128]{3,2,1,0:T(8,128)(2,1)} %get-tuple-element.96.refs_0_) | copy-start | bytes 589828
  77.2 16.7 %collective-permute-start.22 = (bf16[4,2,2,128,128]{4,3,2,1,0:T(8,128)(2,1)S(1)}, bf16[4,2,2,128,128]{4,3,2,1,0:T(8,128)(2,1)S(1)}, u32[]{:S(2)}, u32[]{:S(2)}) collective-permute-start(bf16[4,2,2,128,128]{4,3,2,1,0:T(8,128)(2,1)S(1)} %get-tuple-element.132), channel_id=1, source_target_pairs={{0,8},{4,20},{8,0},{12,28},{16,24},{20,4},{24,16},{28,12},{1,9},{5... | collective-permute-start | bytes 1572872 | tf_op jit(solution)/shard_map/ppermute | solution.py:278
  78.7 15.2 %collective-permute-start.23 = (bf16[4,2,2,128,128]{4,3,2,1,0:T(8,128)(2,1)S(1)}, bf16[4,2,2,128,128]{4,3,2,1,0:T(8,128)(2,1)S(1)}, u32[]{:S(2)}, u32[]{:S(2)}) collective-permute-start(bf16[4,2,2,128,128]{4,3,2,1,0:T(8,128)(2,1)S(1)} %get-tuple-element.132), channel_id=1, source_target_pairs={{0,16},{4,12},{8,24},{12,4},{16,0},{20,28},{24,8},{28,20},{1,17},{... | collective-permute-start | bytes 1572872 | tf_op jit(solution)/shard_map/ppermute | solution.py:278
  80.2 13.7 %collective-permute-start.19 = (bf16[2,2,128,128]{3,2,1,0:T(8,128)(2,1)S(1)}, bf16[2,2,128,128]{3,2,1,0:T(8,128)(2,1)S(1)}, u32[]{:S(2)}, u32[]{:S(2)}) collective-permute-start(bf16[2,2,128,128]{3,2,1,0:T(8,128)(2,1)S(1)} %get-tuple-element.107), channel_id=1, source_target_pairs={{0,1},{1,0},{2,3},{3,2},{4,5},{5,4},{6,7},{7,6},{8,9},{9,8},{10,11... | collective-permute-start | bytes 393224 | tf_op jit(solution)/shard_map/ppermute | solution.py:275
  81.8 12.1 %collective-permute-start.20 = (bf16[2,2,128,128]{3,2,1,0:T(8,128)(2,1)S(1)}, bf16[2,2,128,128]{3,2,1,0:T(8,128)(2,1)S(1)}, u32[]{:S(2)}, u32[]{:S(2)}) collective-permute-start(bf16[2,2,128,128]{3,2,1,0:T(8,128)(2,1)S(1)} %get-tuple-element.108), channel_id=1, source_target_pairs={{0,2},{1,3},{2,0},{3,1},{4,6},{5,7},{6,4},{7,5},{8,10},{9,11},{10,... | collective-permute-start | bytes 393224 | tf_op jit(solution)/shard_map/ppermute | solution.py:275
  83.0 10.8 %collective-permute-start.21 = (bf16[2,2,128,128]{3,2,1,0:T(8,128)(2,1)S(1)}, bf16[2,2,128,128]{3,2,1,0:T(8,128)(2,1)S(1)}, u32[]{:S(2)}, u32[]{:S(2)}) collective-permute-start(bf16[2,2,128,128]{3,2,1,0:T(8,128)(2,1)S(1)} %get-tuple-element.109), channel_id=1, source_target_pairs={{0,3},{1,2},{2,1},{3,0},{4,7},{5,6},{6,5},{7,4},{8,11},{9,10},{10,... | collective-permute-start | bytes 393224 | tf_op jit(solution)/shard_map/ppermute | solution.py:275
  93.8 12.0 %copy-start.4 = (bf16[2,1,128,128]{3,2,1,0:T(8,128)(2,1)}, bf16[2,1,128,128]{3,2,1,0:T(8,128)(2,1)S(1)}, u32[]{:S(2)}) copy-start(bf16[2,1,128,128]{3,2,1,0:T(8,128)(2,1)S(1)} %get-tuple-element.117.refs_4_) | copy-start | bytes 196612
  93.8 12.7 %copy-start.3 = (bf16[2,2,128,128]{3,2,1,0:T(8,128)(2,1)}, bf16[2,2,128,128]{3,2,1,0:T(8,128)(2,1)S(1)}, u32[]{:S(2)}) copy-start(bf16[2,2,128,128]{3,2,1,0:T(8,128)(2,1)S(1)} %collective-permute-done.21.refs_3_) | copy-start | bytes 393220
  93.8 12.6 %copy-start.2 = (bf16[2,2,128,128]{3,2,1,0:T(8,128)(2,1)}, bf16[2,2,128,128]{3,2,1,0:T(8,128)(2,1)S(1)}, u32[]{:S(2)}) copy-start(bf16[2,2,128,128]{3,2,1,0:T(8,128)(2,1)S(1)} %collective-permute-done.20.refs_2_) | copy-start | bytes 393220
  93.9 12.6 %copy-start.1 = (bf16[2,2,128,128]{3,2,1,0:T(8,128)(2,1)}, bf16[2,2,128,128]{3,2,1,0:T(8,128)(2,1)S(1)}, u32[]{:S(2)}) copy-start(bf16[2,2,128,128]{3,2,1,0:T(8,128)(2,1)S(1)} %collective-permute-done.19.refs_1_) | copy-start | bytes 393220
  94.0 12.5 %collective-permute-start.27 = (bf16[2,2,2,128,128]{4,3,2,1,0:T(8,128)(2,1)S(1)}, bf16[2,2,2,128,128]{4,3,2,1,0:T(8,128)(2,1)S(1)}, u32[]{:S(2)}, u32[]{:S(2)}) collective-permute-start(bf16[2,2,2,128,128]{4,3,2,1,0:T(8,128)(2,1)S(1)} %slice.114), channel_id=1, source_target_pairs={{0,16},{4,12},{8,24},{12,4},{16,0},{20,28},{24,8},{28,20},{1,17},{... | collective-permute-start | bytes 786440 | tf_op jit(solution)/shard_map/ppermute | solution.py:278
  94.8 11.7 %collective-permute-start.28 = (bf16[2,2,2,128,128]{4,3,2,1,0:T(8,128)(2,1)S(1)}, bf16[2,2,2,128,128]{4,3,2,1,0:T(8,128)(2,1)S(1)}, u32[]{:S(2)}, u32[]{:S(2)}) collective-permute-start(bf16[2,2,2,128,128]{4,3,2,1,0:T(8,128)(2,1)S(1)} %slice.115), channel_id=1, source_target_pairs={{0,8},{4,20},{8,0},{12,28},{16,24},{20,4},{24,16},{28,12},{1,9},{5... | collective-permute-start | bytes 786440 | tf_op jit(solution)/shard_map/ppermute | solution.py:278
  95.3 10.5 %collective-permute-start.24 = (bf16[2,1,128,128]{3,2,1,0:T(8,128)(2,1)S(1)}, bf16[2,1,128,128]{3,2,1,0:T(8,128)(2,1)S(1)}, u32[]{:S(2)}, u32[]{:S(2)}) collective-permute-start(bf16[2,1,128,128]{3,2,1,0:T(8,128)(2,1)S(1)} %get-tuple-element.118), channel_id=1, source_target_pairs={{0,1},{1,0},{2,3},{3,2},{4,5},{5,4},{6,7},{7,6},{8,9},{9,8},{10,11... | collective-permute-start | bytes 196616 | tf_op jit(solution)/shard_map/ppermute | solution.py:275
  97.1 8.7 %collective-permute-start.25 = (bf16[2,1,128,128]{3,2,1,0:T(8,128)(2,1)S(1)}, bf16[2,1,128,128]{3,2,1,0:T(8,128)(2,1)S(1)}, u32[]{:S(2)}, u32[]{:S(2)}) collective-permute-start(bf16[2,1,128,128]{3,2,1,0:T(8,128)(2,1)S(1)} %get-tuple-element.119), channel_id=1, source_target_pairs={{0,2},{1,3},{2,0},{3,1},{4,6},{5,7},{6,4},{7,5},{8,10},{9,11},{10,... | collective-permute-start | bytes 196616 | tf_op jit(solution)/shard_map/ppermute | solution.py:275
  98.1 7.6 %collective-permute-start.26 = (bf16[2,1,128,128]{3,2,1,0:T(8,128)(2,1)S(1)}, bf16[2,1,128,128]{3,2,1,0:T(8,128)(2,1)S(1)}, u32[]{:S(2)}, u32[]{:S(2)}) collective-permute-start(bf16[2,1,128,128]{3,2,1,0:T(8,128)(2,1)S(1)} %get-tuple-element.120), channel_id=1, source_target_pairs={{0,3},{1,2},{2,1},{3,0},{4,7},{5,6},{6,5},{7,4},{8,11},{9,10},{10,... | collective-permute-start | bytes 196616 | tf_op jit(solution)/shard_map/ppermute | solution.py:275
  110.3 9.0 %copy-start.5 = (bf16[2,1,128,128]{3,2,1,0:T(8,128)(2,1)}, bf16[2,1,128,128]{3,2,1,0:T(8,128)(2,1)S(1)}, u32[]{:S(2)}) copy-start(bf16[2,1,128,128]{3,2,1,0:T(8,128)(2,1)S(1)} %get-tuple-element.124.refs_8_) | copy-start | bytes 196612
  110.3 9.0 %collective-permute-start.29 = (bf16[2,1,128,128]{3,2,1,0:T(8,128)(2,1)S(1)}, bf16[2,1,128,128]{3,2,1,0:T(8,128)(2,1)S(1)}, u32[]{:S(2)}, u32[]{:S(2)}) collective-permute-start(bf16[2,1,128,128]{3,2,1,0:T(8,128)(2,1)S(1)} %get-tuple-element.125), channel_id=1, source_target_pairs={{0,1},{1,0},{2,3},{3,2},{4,5},{5,4},{6,7},{7,6},{8,9},{9,8},{10,11... | collective-permute-start | bytes 196616 | tf_op jit(solution)/shard_map/ppermute | solution.py:275
  111.9 7.4 %collective-permute-start.30 = (bf16[2,1,128,128]{3,2,1,0:T(8,128)(2,1)S(1)}, bf16[2,1,128,128]{3,2,1,0:T(8,128)(2,1)S(1)}, u32[]{:S(2)}, u32[]{:S(2)}) collective-permute-start(bf16[2,1,128,128]{3,2,1,0:T(8,128)(2,1)S(1)} %get-tuple-element.126), channel_id=1, source_target_pairs={{0,2},{1,3},{2,0},{3,1},{4,6},{5,7},{6,4},{7,5},{8,10},{9,11},{10,... | collective-permute-start | bytes 196616 | tf_op jit(solution)/shard_map/ppermute | solution.py:275
  113.2 6.1 %collective-permute-start.31 = (bf16[2,1,128,128]{3,2,1,0:T(8,128)(2,1)S(1)}, bf16[2,1,128,128]{3,2,1,0:T(8,128)(2,1)S(1)}, u32[]{:S(2)}, u32[]{:S(2)}) collective-permute-start(bf16[2,1,128,128]{3,2,1,0:T(8,128)(2,1)S(1)} %get-tuple-element.127), channel_id=1, source_target_pairs={{0,3},{1,2},{2,1},{3,0},{4,7},{5,6},{6,5},{7,4},{8,11},{9,10},{10,... | collective-permute-start | bytes 196616 | tf_op jit(solution)/shard_map/ppermute | solution.py:275
  114.7 5.3 %collective-permute-start.32 = (bf16[4,128,128]{2,1,0:T(8,128)(2,1)S(1)}, bf16[4,128,128]{2,1,0:T(8,128)(2,1)S(1)}, u32[]{:S(2)}, u32[]{:S(2)}) collective-permute-start(bf16[4,128,128]{2,1,0:T(8,128)(2,1)S(1)} %pad_maximum_fusion.3), channel_id=1, source_target_pairs={{0,4},{4,0},{8,12},{12,8},{16,20},{20,16},{24,28},{28,24},{1,5},{5... | collective-permute-start | bytes 393224 | tf_op jit(solution)/shard_map/ppermute | solution.py:278
  114.7 5.3 %collective-permute-start.33 = (bf16[4,128,128]{2,1,0:T(8,128)(2,1)S(1)}, bf16[4,128,128]{2,1,0:T(8,128)(2,1)S(1)}, u32[]{:S(2)}, u32[]{:S(2)}) collective-permute-start(bf16[4,128,128]{2,1,0:T(8,128)(2,1)S(1)} %pad_maximum_fusion.4), channel_id=1, source_target_pairs={{0,4},{4,0},{8,12},{12,8},{16,20},{20,16},{24,28},{28,24},{1,5},{5... | collective-permute-start | bytes 393224 | tf_op jit(solution)/shard_map/ppermute | solution.py:278
  119.3 0.6 copy-start.21
  120.0 1.4 %collective-permute-start.34 = (bf16[4,128,128]{2,1,0:T(8,128)(2,1)S(1)}, bf16[4,128,128]{2,1,0:T(8,128)(2,1)S(1)}, u32[]{:S(2)}, u32[]{:S(2)}) collective-permute-start(bf16[4,128,128]{2,1,0:T(8,128)(2,1)S(1)} %pad_maximum_fusion.5), channel_id=1, source_target_pairs={{0,4},{4,0},{8,12},{12,8},{16,20},{20,16},{24,28},{28,24},{1,5},{5... | collective-permute-start | bytes 393224 | tf_op jit(solution)/shard_map/ppermute | solution.py:278
  120.0 1.3 %copy-start.25 = (bf16[4,128,128]{2,1,0:T(8,128)(2,1)}, bf16[4,128,128]{2,1,0:T(8,128)(2,1)S(1)}, u32[]{:S(2)}) copy-start(bf16[4,128,128]{2,1,0:T(8,128)(2,1)S(1)} %collective-permute-done.32.refs_12_) | copy-start | bytes 393220
  120.0 1.3 %copy-start.26 = (bf16[4,128,128]{2,1,0:T(8,128)(2,1)}, bf16[4,128,128]{2,1,0:T(8,128)(2,1)S(1)}, u32[]{:S(2)}) copy-start(bf16[4,128,128]{2,1,0:T(8,128)(2,1)S(1)} %collective-permute-done.33.refs_13_) | copy-start | bytes 393220
  121.4 0.7 copy-start.27
  (5 other events, 3.1 us)
